TPU v7x, 128 devices: a whole 4x4x4 slice. The times are simulated.
128 devices in a mesh: blk: 4 (over x), pts: 32 (over y, z, core).
Axes of the slice: x: 4, y: 4, z: 4, core: 2. Of those that a mesh axis runs over, the one named last changes fastest.
Arguments:
- snapshots: bfloat16 [4096, 3, 65536], P('blk', None, 'pts'), may hold values from -6 to 6
- tail_rows: bfloat16 [128, 3, 65536], P(None, None, 'pts'), may hold values from -6 to 6
- point_weight: float32 [3, 65536], P(None, 'pts'), may hold values from 0.2 to 2
- freq_bins: int32 [16], replicated, may hold values from 1 to 127
Outputs:
- recon: bfloat16 [16, 2, 32, 3, 65536], P('blk', None, None, None, 'pts')
All inputs are finite; a program needn't handle non-finite values.
Results may differ from a plain program's by a relative error of at most 0.0067.
Values may be sent and summed in bfloat16 or wider, within the bound.
No kernel may reach another device: no remote copies, remote signals or barrier semaphores. Data moves between devices by JAX's collectives and lax.ppermute only.
A program may use at most 192 MiB of HBM per device.

v0:
```python
import math

import jax
import jax.numpy as jnp
from jax import lax
from jax.sharding import PartitionSpec as P

MODES = 4
EIG_ITERS = 3


def shifted(value, axis, steps):
    count = lax.axis_size(axis)
    initial, last = (max(0, -steps), min(count, count - steps))
    return lax.ppermute(value, axis, [(source, source + steps) for source in range(initial, last)])


def fourier_table(freq_bins, length):
    steps = jnp.arange(length, dtype=jnp.int32)
    product = freq_bins[:, None] * steps[None, :] % length
    angle = product.astype(jnp.float32) * (2.0 * math.pi / length)
    window = 0.5 - 0.5 * jnp.cos(steps.astype(jnp.float32) * (2.0 * math.pi / length))
    cosine = window[None, :] * jnp.cos(angle)
    sine = -window[None, :] * jnp.sin(angle)
    return jnp.concatenate([cosine, sine], axis=0).astype(jnp.bfloat16)


def weighted_gram(side_rows, weight):
    values = side_rows.astype(jnp.float32)
    return jnp.dot(values * weight[None, :], values.T, precision=lax.Precision.HIGHEST)


def spectral(gram_matrix, blocks):
    real_part = gram_matrix[:blocks, :blocks] + gram_matrix[blocks:, blocks:]
    imag_part = gram_matrix[:blocks, blocks:] - gram_matrix[blocks:, :blocks]
    upper = jnp.concatenate([real_part, imag_part], axis=1)
    lower = jnp.concatenate([-imag_part, real_part], axis=1)
    return jnp.concatenate([upper, lower], axis=0)


def orthonormal(basis):
    inner = jnp.dot(basis.T, basis, precision=lax.Precision.HIGHEST)
    factor = jnp.linalg.cholesky(inner)
    return lax.linalg.triangular_solve(factor, basis, left_side=False, lower=True, transpose_a=True)


def projector(operator, blocks):
    basis = jnp.concatenate([operator[:, :MODES], operator[:, blocks : blocks + MODES]], axis=1)
    basis = orthonormal(basis)
    for sweep in range(EIG_ITERS):
        basis = orthonormal(jnp.dot(operator, basis, precision=lax.Precision.HIGHEST))
    return jnp.dot(basis, basis.T, precision=lax.Precision.HIGHEST)


def on_device(snapshots, tail_rows, point_weight, freq_bins):
    row_count, comp_count, point_count = snapshots.shape
    half_len = tail_rows.shape[0]
    width = comp_count * point_count
    own_rows = snapshots.reshape(row_count, width)
    tail_flat = tail_rows.reshape(half_len, width)
    is_last = lax.axis_index("blk") == lax.axis_size("blk") - 1
    group_blocks = row_count // half_len
    table = fourier_table(freq_bins, 2 * half_len)
    incoming = shifted(own_rows[:half_len], "blk", -1)
    incoming = jnp.where(is_last, tail_flat, incoming)
    halves = jnp.concatenate([own_rows, incoming], axis=0).reshape(
        group_blocks + 1, half_len, width
    )
    first_part = jnp.einsum(
        "fn,bnq->fbq", table[:, :half_len], halves[:-1], preferred_element_type=jnp.float32
    )
    second_part = jnp.einsum(
        "fn,bnq->fbq", table[:, half_len:], halves[1:], preferred_element_type=jnp.float32
    )
    freq_count = freq_bins.shape[0]
    coefficients = (
        (first_part + second_part).astype(jnp.bfloat16).reshape(2, freq_count, group_blocks, width)
    )
    gathered = lax.all_gather(coefficients, "blk", axis=2, tiled=True)
    local_freqs = freq_count // lax.axis_size("blk")
    mine = lax.dynamic_slice_in_dim(gathered, lax.axis_index("blk") * local_freqs, local_freqs, 1)
    local_freqs = mine.shape[1]
    all_blocks = mine.shape[2]
    weight = point_weight.reshape(-1)
    side_list = [
        mine[:, freq_index].reshape(2 * all_blocks, width) for freq_index in range(local_freqs)
    ]
    gram_list = [lax.psum(weighted_gram(side_rows, weight), "pts") for side_rows in side_list]
    results = []
    for freq_index in range(local_freqs):
        projection = projector(spectral(gram_list[freq_index], all_blocks), all_blocks).astype(
            jnp.bfloat16
        )
        filtered = jnp.dot(
            projection, side_list[freq_index], preferred_element_type=jnp.float32
        ).astype(jnp.bfloat16)
        results.append(filtered.reshape(2, all_blocks, comp_count, point_count))
    return jnp.stack(results, axis=0)


def solution(mesh):
    in_specs = (P("blk", None, "pts"), P(None, None, "pts"), P(None, "pts"), P())
    out_specs = P("blk", None, None, None, "pts")
    return jax.shard_map(
        on_device, mesh=mesh, in_specs=in_specs, out_specs=out_specs, check_vma=False
    )
```

profile of v0, /device:TPU:1, one launch (start us, length us, event | category | flops | bytes accessed | tf_op | source)
XLA Modules:
  0.0 448.9 jit_solution(17900416809572347104)
XLA Ops:
  6.5 16.7 %copy.81 = bf16[1024,3,2048]{0,2,1:T(8,128)(2,1)} copy(bf16[1024,3,2048]{2,0,1:T(8,128)(2,1)} %param.7) | data formatting | bytes 25165824 | tf_op args[0]
  23.2 2.7 slice.149
  25.9 1.3 collective-permute-start
  27.2 18.9 %copy.129 = bf16[1024,3,2048]{2,1,0:T(4,128)(2,1)} copy(bf16[1024,3,2048]{2,0,1:T(8,128)(2,1)} %param.7) | data formatting | bytes 25165824 | tf_op jit(solution)/shard_map/slice | solution.py:70
  46.0 34.5 %reshape.130 = bf16[8,128,6144]{2,1,0:T(8,128)(2,1)} reshape(bf16[1024,3,2048]{2,1,0:T(4,128)(2,1)} %copy.129) | data formatting | bytes 25165824 | tf_op jit(solution)/shard_map/slice | solution.py:70
  80.5 1.9 copy.84
  82.7 9.4 %fusion.9 = f32[32,8,6144]{2,0,1:T(8,128)} fusion(bf16[8,128,6144]{2,1,0:T(8,128)(2,1)} %reshape.130, bf16[16,256]{1,0:T(8,128)(2,1)S(1)} %get-tuple-element.46, bf16[16,256]{1,0:T(8,128)(2,1)S(1)} %get-tuple-element.45), kind=kOutput, calls=%fused_computation.60 | convolution fusion | flops 402669568 | bytes 18890752 | tf_op jit(solution)/shard_map/fn,bnq->fbq/dot_general | solution.py:69
  92.6 5.3 %pad_maximum_fusion = bf16[1024,6144]{0,1:T(8,128)(2,1)} fusion(bf16[128,6144]{0,1:T(8,128)(2,1)S(1)} %bitcast_select_fusion, bf16[1024,6144]{0,1:T(8,128)(2,1)S(1)} %bitcast.300), kind=kLoop, calls=%fused_computation | loop fusion | flops 25165824 | bytes 26738688 | tf_op jit(solution)/shard_map/concatenate | solution.py:66
  97.9 16.7 %copy.86 = bf16[1024,6144]{1,0:T(8,128)(2,1)} copy(bf16[1024,6144]{0,1:T(8,128)(2,1)} %pad_maximum_fusion) | data formatting | bytes 25165824 | tf_op jit(solution)/shard_map/slice | solution.py:73
  114.6 8.1 %fusion = bf16[32,8,6144]{2,0,1:T(8,128)(2,1)S(1)} fusion(f32[32,8,6144]{2,0,1:T(8,128)} %fusion.9, bf16[8,128,6144]{2,1,0:T(8,128)(2,1)} %bitcast.301, bf16[16,256]{1,0:T(8,128)(2,1)S(1)} %get-tuple-element.45, bf16[16,256]{1,0:T(8,128)(2,1)S(1)} %get-tuple-element.46), kind=kOutput, calls=%fused_computation.2 | convolution fusion | flops 405815296 | bytes 22036480 | tf_op jit(solution)/shard_map/fn,bnq->fbq/dot_general | solution.py:72
  122.7 3.4 copy.87
  126.9 122.4 %all-gather.2.cloned.1.call-done = bf16[2,16,32,6144]{3,2,0,1:T(8,128)(2,1)} async-done(((bf16[2,16,8,6144]{3,2,0,1:T(8,128)(2,1)}), bf16[2,16,32,6144]{3,2,0,1:T(8,128)(2,1)}) %all-gather.2.cloned.1.call-update) | async-done | bytes 12582928 | tf_op jit(solution)/shard_map/all_gather | solution.py:79
  249.3 2.8 convert_multiply_fusion.3
  252.1 1.5 fusion.91
  253.6 1.5 fusion.98
  255.1 1.5 fusion.105
  256.6 1.5 fusion.112
  258.1 101.2 %all-reduce.3.cloned.1.call-done = (f32[64,64]{1,0:T(8,128)}, f32[64,64]{1,0:T(8,128)}, f32[64,64]{1,0:T(8,128)}, f32[64,64]{1,0:T(8,128)}) async-done(((f32[64,64]{1,0:T(8,128)}, f32[64,64]{1,0:T(8,128)}, f32[64,64]{1,0:T(8,128)}, f32[64,64]{1,0:T(8,128)}), (f32[64,64]{1,0:T(8,128)}, f32[64,64]{1,0:T(8,128)}, f32[64,64]{1,0:T(8,128)}, f32[64,64]{1,0:T(8,128)})) %all-reduce.3.cloned.1.call-update) | async-done | bytes 65552 | tf_op jit(solution)/shard_map/psum | solution.py:88
  359.3 0.9 fusion.83
  360.7 0.7 cholesky.254
  361.5 0.6 compare_reduce_fusion.15
  362.1 0.6 fusion.14
  364.0 0.7 cholesky.265
  365.4 0.6 fusion.15
  367.3 0.7 cholesky.276
  368.7 0.6 fusion.16
  370.6 0.7 cholesky.287
  372.0 0.6 fusion.17
  373.7 1.2 convolution_convert_fusion.3
  374.9 2.7 stack_reshape.12
  378.3 0.7 cholesky.298
  379.7 0.6 fusion.18
  381.6 0.7 cholesky.309
  383.0 0.6 fusion.19
  384.9 0.7 cholesky.320
  386.3 0.6 fusion.20
  388.1 0.7 cholesky.331
  389.6 0.6 fusion.21
  391.3 1.2 convolution_convert_fusion.2
  392.5 3.6 stack_reshape.13
  396.7 0.7 cholesky.342
  397.5 0.6 compare_reduce_fusion.7
  398.1 0.6 fusion.22
  400.0 0.7 cholesky.353
  400.8 0.6 compare_reduce_fusion.6
  401.4 0.6 fusion.23
  403.3 0.7 cholesky.364
  404.7 0.6 fusion.24
  406.6 0.7 cholesky.375
  408.0 0.6 fusion.25
  409.7 1.2 convolution_convert_fusion.1
  410.9 3.7 stack_reshape.14
  415.2 0.7 cholesky.386
  416.6 0.6 fusion.26
  418.5 0.7 cholesky.397
  419.9 0.6 fusion.27
  421.8 0.7 cholesky.408
  423.2 0.6 fusion.28
  425.1 0.7 cholesky.419
  426.5 0.6 fusion.29
  428.2 1.3 convolution_convert_fusion
  429.5 3.6 stack_reshape.15
  433.1 5.0 %pad_maximum_fusion.1 = bf16[4,2,32,3,2048]{4,3,2,1,0:T(4,128)(2,1)S(1)} fusion(bf16[1,2,32,3,2048]{4,3,2,1,0:T(4,128)(2,1)} %stack_reshape.15, bf16[1,2,32,3,2048]{4,3,2,1,0:T(4,128)(2,1)} %stack_reshape.14, bf16[1,2,32,3,2048]{4,3,2,1,0:T(4,128)(2,1)S(1)} %copy-done, bf16[1,2,32,3,2048]{4,3,2,1,0:T(4,128)(2,1)S(1)} %stack_reshape.12), kind=kLoop, calls=%fused_computation.7 | loop fusion | flops 4718592 | bytes 6291456 | tf_op jit(solution)/shard_map/stack | solution.py:98
  438.0 4.0 copy.128
  (172 shorter events, 32.1 us)
Async XLA Ops:
  6.5 242.8 %all-gather.2.cloned.1.call-start = ((), (), s32[]{:S(2)}) async-start(), calls=%async_computation | async-start | bytes 15728640 | tf_op jit(solution)/shard_map/all_gather | solution.py:79
  25.9 66.2 %collective-permute-start = (bf16[128,6144]{0,1:T(8,128)(2,1)}, bf16[128,6144]{0,1:T(8,128)(2,1)S(1)}, u32[]{:S(2)}, u32[]{:S(2)}) collective-permute-start(bf16[128,6144]{0,1:T(8,128)(2,1)} %bitcast.4), channel_id=1, source_target_pairs={{32,0},{64,32},{96,64},{33,1},{65,33},{97,65},{34,2},{66,34},{98,6... | collective-permute-start | bytes 4718600 | tf_op jit(solution)/shard_map/ppermute | solution.py:15
  80.5 2.0 copy-start.5
  82.6 9.7 %slice-start = ((s8[12582912]{0:T(1024)(128)(4,1)}), s8[4194304]{0:T(1024)(128)(4,1)S(1)}, s32[]{:S(2)}) async-start(s8[12582912]{0:T(1024)(128)(4,1)} %bitcast.298), calls=%async_computation.2 | async-start | bytes 8388608
  82.6 9.7 %slice-start.1 = ((s8[12582912]{0:T(1024)(128)(4,1)}), s8[4194304]{0:T(1024)(128)(4,1)S(1)}, s32[]{:S(2)}) async-start(s8[12582912]{0:T(1024)(128)(4,1)} %bitcast.298), calls=%async_computation.3 | async-start | bytes 8388608
  82.6 9.9 %slice-start.2 = ((s8[12582912]{0:T(1024)(128)(4,1)}), s8[4194304]{0:T(1024)(128)(4,1)S(1)}, s32[]{:S(2)}) async-start(s8[12582912]{0:T(1024)(128)(4,1)} %bitcast.298), calls=%async_computation.4 | async-start | bytes 8388608
  126.1 0.8 copy-start.4
  126.1 233.2 %all-reduce.3.cloned.1.call-start = ((), (), s32[]{:S(2)}) async-start(), calls=%async_computation.1 | async-start | bytes 262144 | tf_op jit(solution)/shard_map/psum | solution.py:88
  359.3 18.4 %copy-start.3 = (f32[64,64]{1,0:T(8,128)S(1)}, f32[64,64]{1,0:T(8,128)}, u32[]{:S(2)}) copy-start(f32[64,64]{1,0:T(8,128)} %get-tuple-element.9) | copy-start | bytes 49156
  374.9 21.2 %copy-start.2 = (f32[64,64]{1,0:T(8,128)S(1)}, f32[64,64]{1,0:T(8,128)}, u32[]{:S(2)}) copy-start(f32[64,64]{1,0:T(8,128)} %get-tuple-element.8) | copy-start | bytes 49156
  392.5 22.1 %copy-start.1 = (f32[64,64]{1,0:T(8,128)S(1)}, f32[64,64]{1,0:T(8,128)}, u32[]{:S(2)}) copy-start(f32[64,64]{1,0:T(8,128)} %get-tuple-element.6) | copy-start | bytes 49156
  410.9 22.1 %copy-start = (bf16[1,2,32,3,2048]{4,3,2,1,0:T(4,128)(2,1)S(1)}, bf16[1,2,32,3,2048]{4,3,2,1,0:T(4,128)(2,1)}, u32[]{:S(2)}) copy-start(bf16[1,2,32,3,2048]{4,3,2,1,0:T(4,128)(2,1)} %stack_reshape.13) | copy-start | bytes 2359300
Sparse Core Ops, SparseCore 0:
  126.3 123.0 all-gather.1
  258.2 101.0 all-reduce.2
where the time goes:
time: 451 us; the launch traced here: 449 us
  waiting for transfers between devices  224 us (50%)
  local copies, waits for them, and re-layouts  115 us (25%)
  other arithmetic  58 us (13%)
  matrix products  36.9 us (8%)
  between operations  13.8 us (3%)
    all_gather x1, waiting for transfers between devices, on_device(): gathered = lax.all_gather(coefficients, 'blk', axis=2, tiled=True)  122 us
    psum x1, waiting for transfers between devices, on_device(): lax.psum(weighted_gram(side_rows, weight), 'pts')  101 us
    slice x2, local copies, waits for them, and re-layouts, on_device(): halves[:-1]  53.3 us
    another operation x48, other arithmetic, orthonormal(): factor = jnp.linalg.cholesky(inner)  22.5 us
    another operation x32, other arithmetic, orthonormal(): lax.linalg.triangular_solve(factor, basis, left_side=False, lower=True, t...  20.4 us
    unnamed x20, local copies, waits for them, and re-layouts  19.3 us
    another operation x5, local copies, waits for them, and re-layouts, on_device(): return jnp.stack(results, axis=0)  17.5 us
    slice x1, local copies, waits for them, and re-layouts, on_device(): halves[1:]  16.7 us
  transfers between devices with their start and end apart: 3, of which 2 were waited for; matrix products, arithmetic and copies ran while one was open for 14% of the time, Pallas kernels for 0%

commit v1 on v0

v1 whole, which is shorter than its diff:
```python
import functools
import math

import jax
import jax.numpy as jnp
from jax import lax
from jax.experimental import pallas as pl
from jax.experimental.pallas import tpu as pltpu
from jax.sharding import PartitionSpec as P

MODES = 4
EIG_ITERS = 3
TILE = 512
CHUNKS = (1, 3, 4, 3, 1)
HIGHEST = lax.Precision.HIGHEST


def fourier_table(freq_bins, length):
    steps = jnp.arange(length, dtype=jnp.int32)
    product = freq_bins[:, None] * steps[None, :] % length
    angle = product.astype(jnp.float32) * (2.0 * math.pi / length)
    window = 0.5 - 0.5 * jnp.cos(steps.astype(jnp.float32) * (2.0 * math.pi / length))
    cosine = window[None, :] * jnp.cos(angle)
    sine = -window[None, :] * jnp.sin(angle)
    table = jnp.stack([cosine, sine], axis=1).astype(jnp.bfloat16)
    return table.reshape(2 * freq_bins.shape[0], length)


def banded(table, blocks):
    rows, length = table.shape
    half = length // 2
    block = lax.broadcasted_iota(jnp.int32, (rows, blocks, blocks, half), 1)
    part = lax.broadcasted_iota(jnp.int32, (rows, blocks, blocks, half), 2)
    first = table[:, None, None, :half]
    second = table[:, None, None, half:]
    zero = jnp.zeros((), table.dtype)
    full = jnp.where(part == block, first, jnp.where(part == block + 1, second, zero))
    return full.reshape(rows * blocks, blocks * half)


def fourier_kernel(me_ref, band_ref, edge_ref, x_ref, tail_ref, *outs):
    main = jnp.dot(band_ref[...], x_ref[0], preferred_element_type=jnp.float32)
    main = main.astype(jnp.bfloat16)
    size = main.shape[0] // len(outs)
    half = tail_ref.shape[1]
    for peer, out in enumerate(outs):
        out[:size, :] = main[peer * size : (peer + 1) * size]

    def edge(rows):
        result = jnp.dot(edge_ref[...], rows, preferred_element_type=jnp.float32)
        result = result.astype(jnp.bfloat16)
        step = result.shape[0] // len(outs)
        for peer, out in enumerate(outs):
            out[size:, :] = result[peer * step : (peer + 1) * step]

    @pl.when(me_ref[0] == 0)
    def _():
        edge(tail_ref[0])

    @pl.when(me_ref[0] != 0)
    def _():
        edge(x_ref[0, :half, :])


def fourier(me, band, edge, snapshots, tail, first_tile, tiles):
    comps, rows, points = snapshots.shape
    half = tail.shape[1]
    per_comp = points // TILE
    size = band.shape[0] // 4 + edge.shape[0] // 4

    def place(t):
        return ((t + first_tile) // per_comp, 0, (t + first_tile) % per_comp)

    return pl.pallas_call(
        fourier_kernel,
        grid=(tiles,),
        in_specs=[
            pl.BlockSpec(memory_space=pltpu.SMEM),
            pl.BlockSpec(band.shape, lambda t: (0, 0)),
            pl.BlockSpec(edge.shape, lambda t: (0, 0)),
            pl.BlockSpec((1, rows, TILE), place),
            pl.BlockSpec((1, half, TILE), place),
        ],
        out_specs=[pl.BlockSpec((size, TILE), lambda t: (0, t))] * 4,
        out_shape=[jax.ShapeDtypeStruct((size, tiles * TILE), jnp.bfloat16)] * 4,
        compiler_params=pltpu.CompilerParams(vmem_limit_bytes=48 * 2**20),
        cost_estimate=pl.CostEstimate(
            flops=2 * band.shape[0] * rows * tiles * TILE,
            bytes_accessed=2 * (rows + half + 4 * size) * tiles * TILE,
            transcendentals=0,
        ),
        name="fourier",
    )(me, band, edge, snapshots, tail)


def gram_kernel(me_ref, weight_ref, *refs):
    parts, refs = refs[:4], refs[4:]
    total_in = refs[0] if len(refs) == 5 else None
    total_ref, side_ref, total = refs[-3:]
    step = pl.program_id(0)
    me = me_ref[0]

    @pl.when(step == 0)
    def _():
        total[...] = jnp.zeros_like(total)

    last = lax.broadcasted_iota(jnp.int32, (8, TILE), 0) == 7
    for peer in range(4):
        group = lax.rem(me - peer + 4, 4)
        rows = parts[peer][:64, :].astype(jnp.float32)
        edge = parts[(peer - 1) % 4][64:72, :].astype(jnp.float32)
        pieces = [
            rows[8 * k : 8 * k + 8] + jnp.where(last, edge[k : k + 1], 0.0) for k in range(8)
        ]
        for freq in range(4):
            both = jnp.concatenate(pieces[2 * freq : 2 * freq + 2], axis=0)
            start = pl.multiple_of(64 * freq + 16 * group, 16)
            side_ref[pl.ds(start, 16), :] = both.astype(jnp.bfloat16)
    side = side_ref[...]
    scaled = side.astype(jnp.float32) * weight_ref[...]
    high = scaled.astype(jnp.bfloat16)
    low = (scaled - high.astype(jnp.float32)).astype(jnp.bfloat16)
    dims = (((1,), (1,)), ((), ()))
    total[...] += lax.dot_general(
        high, side, dims, preferred_element_type=jnp.float32
    ) + lax.dot_general(low, side, dims, preferred_element_type=jnp.float32)

    @pl.when(step == pl.num_programs(0) - 1)
    def _():
        lane = lax.broadcasted_iota(jnp.int32, (8, 128), 1)
        real_lane = lax.rem(lane, 16) < 8
        low_lane = lane < 64
        for pair in range(2):
            for group in range(4):
                tops = []
                for freq in (2 * pair, 2 * pair + 1):
                    start = 64 * freq + 16 * group
                    columns = slice(128 * pair, 128 * pair + 128)
                    real = total[start : start + 8, columns]
                    imag = total[start + 8 : start + 16, columns]
                    turned = jnp.where(
                        real_lane, pltpu.roll(imag, 120, 1), -pltpu.roll(imag, 8, 1)
                    )
                    tops.append(real + turned)
                rows = slice(32 * pair + 8 * group, 32 * pair + 8 * group + 8)
                top = jnp.where(low_lane, tops[0], tops[1])
                total_ref[rows, :] = top if total_in is None else top + total_in[rows, :]


def gram(me, weight, parts, before, first_tile, tiles):
    size = parts[0].shape[0]
    width = weight.shape[1]
    before_specs = [pl.BlockSpec((64, 128), lambda t: (0, 0)), pl.BlockSpec(memory_space=pl.ANY)]
    return pl.pallas_call(
        gram_kernel,
        grid=(tiles,),
        in_specs=[
            pl.BlockSpec(memory_space=pltpu.SMEM),
            pl.BlockSpec((1, TILE), lambda t: (0, t + first_tile)),
        ]
        + [pl.BlockSpec((size, TILE), lambda t: (0, t))] * 4
        + before_specs[: len(before)],
        out_specs=[
            pl.BlockSpec((64, 128), lambda t: (0, 0)),
            pl.BlockSpec((256, TILE), lambda t: (0, t + first_tile)),
        ],
        out_shape=[
            jax.ShapeDtypeStruct((64, 128), jnp.float32),
            jax.ShapeDtypeStruct((256, width), jnp.bfloat16),
        ],
        scratch_shapes=[pltpu.VMEM((256, 256), jnp.float32)],
        input_output_aliases={7: 1} if before else {},
        compiler_params=pltpu.CompilerParams(vmem_limit_bytes=32 * 2**20),
        cost_estimate=pl.CostEstimate(
            flops=4 * 256 * 256 * tiles * TILE,
            bytes_accessed=2 * (4 * size + 256) * tiles * TILE,
            transcendentals=0,
        ),
        name="gram",
    )(me, weight, *parts, *before)


def projections(total_ref, proj_ref):
    lane = lax.broadcasted_iota(jnp.int32, (8, 128), 1)
    row = lax.broadcasted_iota(jnp.int32, (8, 128), 0)
    real_lane = lax.rem(lane, 16) < 8
    low_lane = lane < 64
    low_row = row < 4
    own_lane = low_row == low_lane
    place = lax.rem(row, 4)

    def turn(value):
        return jnp.where(real_lane, -pltpu.roll(value, 120, 1), pltpu.roll(value, 8, 1))

    def pick(value, j):
        return jnp.where(low_row, value[j : j + 1], value[4 + j : 5 + j])

    def orthonormal(base):
        other = turn(base)
        for j in range(MODES):
            one, two = pick(base, j), pick(other, j)
            along = jnp.sum(base * one, axis=1, keepdims=True)
            across = jnp.sum(base * two, axis=1, keepdims=True)
            norm = pick(along, j)
            inverse = 1.0 / norm
            a, b = along * inverse, across * inverse
            scale = lax.rsqrt(norm)
            later = place > j
            new_base = jnp.where(later, base - a * one - b * two, base)
            new_other = jnp.where(later, other - a * two + b * one, other)
            here = place == j
            base = jnp.where(here, base * scale, new_base)
            other = jnp.where(here, other * scale, new_other)
        return base, other

    for pair in range(2):
        blocks = [total_ref[32 * pair + 8 * g : 32 * pair + 8 * g + 8, :] for g in range(4)]
        operator = []
        for keep in (low_lane, jnp.logical_not(low_lane)):
            for block in blocks:
                top = jnp.where(keep, block, 0.0)
                operator += [top, turn(top)]
        operator = jnp.concatenate(operator, axis=0)
        first = blocks[0]
        base = jnp.where(low_row, first, pltpu.roll(first, 4, 0))
        base = jnp.where(own_lane, base, 0.0)
        base, other = orthonormal(base)
        for sweep in range(EIG_ITERS):
            base = jnp.dot(base, operator, precision=HIGHEST, preferred_element_type=jnp.float32)
            base, other = orthonormal(base)
        both = jnp.concatenate([base, other], axis=0)
        whole = lax.dot_general(
            both, both, (((0,), (0,)), ((), ())), precision=HIGHEST,
            preferred_element_type=jnp.float32,
        )
        rows = []
        for freq in range(2):
            for part in range(2):
                for group in range(4):
                    start = 64 * freq + 16 * group + 8 * part
                    rows.append(whole[start : start + 8])
        proj_ref[pair] = jnp.concatenate(rows, axis=0).astype(jnp.bfloat16)


def recon_kernel(total_ref, side_ref, out_ref, proj_ref):
    @pl.when(pl.program_id(0) == 0)
    def _():
        projections(total_ref, proj_ref)

    for pair in range(2):
        result = jnp.dot(
            proj_ref[pair],
            side_ref[128 * pair : 128 * pair + 128, :],
            preferred_element_type=jnp.float32,
        ).astype(jnp.bfloat16)
        for freq in range(2):
            for part in range(2):
                start = 64 * freq + 32 * part
                out_ref[2 * pair + freq, part, 0] = result[start : start + 32]


def recon(total, side, comps, points):
    tile = 1024
    per_comp = points // tile
    return pl.pallas_call(
        recon_kernel,
        grid=(comps * per_comp,),
        in_specs=[
            pl.BlockSpec(total.shape, lambda t: (0, 0)),
            pl.BlockSpec((256, tile), lambda t: (0, t)),
        ],
        out_specs=pl.BlockSpec(
            (4, 2, 1, 32, tile), lambda t: (0, 0, t // per_comp, 0, t % per_comp)
        ),
        out_shape=jax.ShapeDtypeStruct((4, 2, comps, 32, points), jnp.bfloat16),
        scratch_shapes=[pltpu.VMEM((2, 128, 128), jnp.bfloat16)],
        compiler_params=pltpu.CompilerParams(vmem_limit_bytes=32 * 2**20),
        name="recon",
    )(total, side)


def point_sum(value):
    def moved(array, dy, dz, dc):
        def index(y, z, c):
            return (y % 4) * 8 + (z % 4) * 2 + c % 2

        pairs = [
            (index(y, z, c), index(y + dy, z + dz, c + dc))
            for y in range(4)
            for z in range(4)
            for c in range(2)
        ]
        return lax.ppermute(array, "pts", pairs)

    value = value + moved(value, 0, 0, 1)
    value = value + moved(value, 0, 1, 0) + moved(value, 0, -1, 0) + moved(value, 0, 2, 0)
    return value + moved(value, 1, 0, 0) + moved(value, -1, 0, 0) + moved(value, 2, 0, 0)


def on_device(snapshots, tail_rows, point_weight, freq_bins):
    row_count, comps, points = snapshots.shape
    half = tail_rows.shape[0]
    snapshots = jnp.transpose(snapshots, (1, 0, 2))
    tail = jnp.transpose(tail_rows, (1, 0, 2))
    weight = point_weight.reshape(1, comps * points)
    position = lax.axis_index("blk")
    me = position.astype(jnp.int32).reshape(1)
    freq_count = freq_bins.shape[0]
    own = freq_count // 4
    turned = lax.dynamic_slice(jnp.concatenate([freq_bins, freq_bins]), (own * position,), (freq_count,))
    table = fourier_table(turned, 2 * half)
    band = banded(table, row_count // half)
    edge = table[:, half:]
    arrived = []
    starts = [sum(CHUNKS[:k]) for k in range(len(CHUNKS))]
    for start, tiles in zip(starts, CHUNKS):
        sent = fourier(me, band, edge, snapshots, tail, start, tiles)
        parts = [sent[0]]
        for shift in range(1, 4):
            pairs = [(k, (k + shift) % 4) for k in range(4)]
            parts.append(lax.ppermute(sent[shift], "blk", pairs))
        arrived.append(parts)
    before = ()
    for start, tiles, parts in zip(starts, CHUNKS, arrived):
        before = gram(me, weight, parts, before, start, tiles)
    total, side = before
    total = point_sum(total)
    out = recon(total, side, comps, points)
    return jnp.transpose(out, (0, 1, 3, 2, 4))


def solution(mesh):
    in_specs = (P("blk", None, "pts"), P(None, None, "pts"), P(None, "pts"), P())
    out_specs = P("blk", None, None, None, "pts")
    return jax.shard_map(
        on_device, mesh=mesh, in_specs=in_specs, out_specs=out_specs, check_vma=False
    )
```

time: 451 us -> 87.6 us (0.19)
  the two profiles are of different devices: /device:TPU:1 before, /device:TPU:0 now
where the time goes in v1:
time: 87.6 us; the launch traced here: 87.2 us
  starting transfers between devices  34.3 us (39%)
  Pallas kernels  30.3 us (35%)
  waiting for transfers between devices  19.2 us (22%)
  local copies, waits for them, and re-layouts  1.73 us (2%)
  other arithmetic  1.39 us (2%)
    ppermute x15, starting transfers between devices, on_device(): parts.append(lax.ppermute(sent[shift], 'blk', pairs))  23.1 us
    pallas_call x5, Pallas kernels, fourier(): pl.pallas_call(fourier_kernel, grid=(tiles,), in_specs=[pl.BlockSpec(memo...  15.4 us
    ppermute x7, starting transfers between devices, moved(): return lax.ppermute(array, 'pts', pairs)  11.3 us
    ppermute x15, waiting for transfers between devices, on_device(): parts.append(lax.ppermute(sent[shift], 'blk', pairs))  10.9 us
    pallas_call x1, Pallas kernels, recon(): pl.pallas_call(recon_kernel, grid=(comps * per_comp,), in_specs=[pl.Block...  8.42 us
    ppermute x7, waiting for transfers between devices, moved(): return lax.ppermute(array, 'pts', pairs)  8.26 us
    pallas_call x5, Pallas kernels, gram(): pl.pallas_call(gram_kernel, grid=(tiles,), in_specs=[pl.BlockSpec(memory_...  6.47 us
  transfers between devices with their start and end apart: 22, of which 6 were waited for; matrix products, arithmetic and copies ran while one was open for 0% of the time, Pallas kernels for 20%

profile of v1, /device:TPU:0, one launch (start us, length us, event | category | flops | bytes accessed | tf_op | source)
XLA Modules:
  0.0 87.2 jit_solution(4467657963260994284)
XLA Ops:
  0.1 0.8 pad_add_fusion
  0.9 0.1 dynamic_slice.3
  1.0 0.2 multiply_convert_fusion.1
  1.2 0.1 iota.62
  1.3 0.1 iota.57
  1.4 0.3 compare_select_fusion.1.band_ref
  1.7 0.0 copy-start
  1.7 1.4 %copy-done = bf16[128,3,2048]{2,0,1:T(8,128)(2,1)S(1)} copy-done((bf16[128,3,2048]{2,0,1:T(8,128)(2,1)S(1)}, bf16[128,3,2048]{2,0,1:T(8,128)(2,1)}, u32[]{:S(2)}) %copy-start) | copy-done | bytes 1572888
  3.1 3.7 %fourier.8 = (bf16[72,1536]{1,0:T(8,128)(2,1)S(1)}, bf16[72,1536]{1,0:T(8,128)(2,1)S(1)}, bf16[72,1536]{1,0:T(8,128)(2,1)S(1)}, bf16[72,1536]{1,0:T(8,128)(2,1)S(1)}) custom-call(s32[1]{0:T(128)} %bitcast.me_ref, bf16[256,1024]{1,0:T(8,128)(2,1)S(1)} %compare_select_fusion.1.band_ref, bf16[32,128]{1,0:T(8,128)(2,1)S(1)} %get-tuple-element.66.edge_ref, ...), custom_call_target="tpu_custom_call" | custom-call | flops 805306368 | bytes 4423680 | tf_op jit(solution)/shard_map/fourier/pallas_call | solution.py:74
  6.8 3.2 %collective-permute-start.10 = (bf16[72,1536]{1,0:T(8,128)(2,1)S(1)}, bf16[72,1536]{1,0:T(8,128)(2,1)S(1)}, u32[]{:S(2)}, u32[]{:S(2)}) collective-permute-start(bf16[72,1536]{1,0:T(8,128)(2,1)S(1)} %get-tuple-element.49), channel_id=1, source_target_pairs={{0,64},{32,96},{64,0},{96,32},{1,65},{33,97},{65,1},{97,33},{2,66}... | collective-permute-start | bytes 663560 | tf_op jit(solution)/shard_map/ppermute | solution.py:321
  10.1 1.1 %collective-permute-start.11 = (bf16[72,1536]{1,0:T(8,128)(2,1)S(1)}, bf16[72,1536]{1,0:T(8,128)(2,1)S(1)}, u32[]{:S(2)}, u32[]{:S(2)}) collective-permute-start(bf16[72,1536]{1,0:T(8,128)(2,1)S(1)} %get-tuple-element.50), channel_id=1, source_target_pairs={{0,96},{32,0},{64,32},{96,64},{1,97},{33,1},{65,33},{97,65},{2,98}... | collective-permute-start | bytes 663560 | tf_op jit(solution)/shard_map/ppermute | solution.py:321
  11.2 1.8 %fourier.9 = (bf16[72,512]{1,0:T(8,128)(2,1)S(1)}, bf16[72,512]{1,0:T(8,128)(2,1)S(1)}, bf16[72,512]{1,0:T(8,128)(2,1)S(1)}, bf16[72,512]{1,0:T(8,128)(2,1)S(1)}) custom-call(s32[1]{0:T(128)} %bitcast.me_ref, bf16[256,1024]{1,0:T(8,128)(2,1)S(1)} %compare_select_fusion.1.band_ref, bf16[32,128]{1,0:T(8,128)(2,1)S(1)} %get-tuple-element.66.edge_ref, ...), custom_call_target="tpu_custom_call" | custom-call | flops 268435456 | bytes 1474560 | tf_op jit(solution)/shard_map/fourier/pallas_call | solution.py:74
  13.0 0.9 %collective-permute-start.12 = (bf16[72,512]{1,0:T(8,128)(2,1)S(1)}, bf16[72,512]{1,0:T(8,128)(2,1)S(1)}, u32[]{:S(2)}, u32[]{:S(2)}) collective-permute-start(bf16[72,512]{1,0:T(8,128)(2,1)S(1)} %get-tuple-element.52), channel_id=1, source_target_pairs={{0,32},{32,64},{64,96},{96,0},{1,33},{33,65},{65,97},{97,1},{2,34}... | collective-permute-start | bytes 221192 | tf_op jit(solution)/shard_map/ppermute | solution.py:321
  13.9 0.7 collective-permute-start.13
  14.6 2.5 %collective-permute-start.14 = (bf16[72,512]{1,0:T(8,128)(2,1)S(1)}, bf16[72,512]{1,0:T(8,128)(2,1)S(1)}, u32[]{:S(2)}, u32[]{:S(2)}) collective-permute-start(bf16[72,512]{1,0:T(8,128)(2,1)S(1)} %get-tuple-element.54), channel_id=1, source_target_pairs={{0,96},{32,0},{64,32},{96,64},{1,97},{33,1},{65,33},{97,65},{2,98}... | collective-permute-start | bytes 221192 | tf_op jit(solution)/shard_map/ppermute | solution.py:321
  17.2 3.7 %fourier.6 = (bf16[72,1536]{1,0:T(8,128)(2,1)S(1)}, bf16[72,1536]{1,0:T(8,128)(2,1)S(1)}, bf16[72,1536]{1,0:T(8,128)(2,1)S(1)}, bf16[72,1536]{1,0:T(8,128)(2,1)S(1)}) custom-call(s32[1]{0:T(128)} %bitcast.me_ref, bf16[256,1024]{1,0:T(8,128)(2,1)S(1)} %compare_select_fusion.1.band_ref, bf16[32,128]{1,0:T(8,128)(2,1)S(1)} %get-tuple-element.66.edge_ref, ...), custom_call_target="tpu_custom_call" | custom-call | flops 805306368 | bytes 4423680 | tf_op jit(solution)/shard_map/fourier/pallas_call | solution.py:74
  20.9 0.0 collective-permute-done.12.refs_1_
  20.9 0.1 collective-permute-start.9
  21.0 0.0 collective-permute-done.13.refs_2_
  21.0 0.0 copy-start.1
  21.0 3.5 %collective-permute-start.3 = (bf16[72,1536]{1,0:T(8,128)(2,1)S(1)}, bf16[72,1536]{1,0:T(8,128)(2,1)S(1)}, u32[]{:S(2)}, u32[]{:S(2)}) collective-permute-start(bf16[72,1536]{1,0:T(8,128)(2,1)S(1)} %get-tuple-element.40), channel_id=1, source_target_pairs={{0,32},{32,64},{64,96},{96,0},{1,33},{33,65},{65,97},{97,1},{2,34}... | collective-permute-start | bytes 663560 | tf_op jit(solution)/shard_map/ppermute | solution.py:321
  24.5 4.4 %fourier.7 = (bf16[72,2048]{1,0:T(8,128)(2,1)S(1)}, bf16[72,2048]{1,0:T(8,128)(2,1)S(1)}, bf16[72,2048]{1,0:T(8,128)(2,1)S(1)}, bf16[72,2048]{1,0:T(8,128)(2,1)S(1)}) custom-call(s32[1]{0:T(128)} %bitcast.me_ref, bf16[256,1024]{1,0:T(8,128)(2,1)S(1)} %compare_select_fusion.1.band_ref, bf16[32,128]{1,0:T(8,128)(2,1)S(1)} %get-tuple-element.66.edge_ref, ...), custom_call_target="tpu_custom_call" | custom-call | flops 1073741824 | bytes 5898240 | tf_op jit(solution)/shard_map/fourier/pallas_call | solution.py:74
  28.9 0.0 collective-permute-done.14.refs_3_
  28.9 0.1 collective-permute-start.6
  29.1 0.0 collective-permute-done.10.refs_2_
  29.1 2.8 %collective-permute-start.7 = (bf16[72,2048]{1,0:T(8,128)(2,1)S(1)}, bf16[72,2048]{1,0:T(8,128)(2,1)S(1)}, u32[]{:S(2)}, u32[]{:S(2)}) collective-permute-start(bf16[72,2048]{1,0:T(8,128)(2,1)S(1)} %get-tuple-element.45), channel_id=1, source_target_pairs={{0,64},{32,96},{64,0},{96,32},{1,65},{33,97},{65,1},{97,33},{2,66}... | collective-permute-start | bytes 884744 | tf_op jit(solution)/shard_map/ppermute | solution.py:321
  31.9 0.0 collective-permute-done.11.refs_3_
  31.9 2.5 %collective-permute-start.8 = (bf16[72,2048]{1,0:T(8,128)(2,1)S(1)}, bf16[72,2048]{1,0:T(8,128)(2,1)S(1)}, u32[]{:S(2)}, u32[]{:S(2)}) collective-permute-start(bf16[72,2048]{1,0:T(8,128)(2,1)S(1)} %get-tuple-element.46), channel_id=1, source_target_pairs={{0,96},{32,0},{64,32},{96,64},{1,97},{33,1},{65,33},{97,65},{2,98}... | collective-permute-start | bytes 884744 | tf_op jit(solution)/shard_map/ppermute | solution.py:321
  34.4 0.0 collective-permute-done.9.refs_1_
  34.4 0.7 collective-permute-start.4
  35.2 0.0 collective-permute-done.3.refs_1_
  35.2 1.4 %collective-permute-start.5 = (bf16[72,1536]{1,0:T(8,128)(2,1)S(1)}, bf16[72,1536]{1,0:T(8,128)(2,1)S(1)}, u32[]{:S(2)}, u32[]{:S(2)}) collective-permute-start(bf16[72,1536]{1,0:T(8,128)(2,1)S(1)} %get-tuple-element.42), channel_id=1, source_target_pairs={{0,96},{32,0},{64,32},{96,64},{1,97},{33,1},{65,33},{97,65},{2,98}... | collective-permute-start | bytes 663560 | tf_op jit(solution)/shard_map/ppermute | solution.py:321
  36.6 1.8 %fourier.5 = (bf16[72,512]{1,0:T(8,128)(2,1)S(1)}, bf16[72,512]{1,0:T(8,128)(2,1)S(1)}, bf16[72,512]{1,0:T(8,128)(2,1)S(1)}, bf16[72,512]{1,0:T(8,128)(2,1)S(1)}) custom-call(s32[1]{0:T(128)} %bitcast.me_ref, bf16[256,1024]{1,0:T(8,128)(2,1)S(1)} %compare_select_fusion.1.band_ref, bf16[32,128]{1,0:T(8,128)(2,1)S(1)} %get-tuple-element.66.edge_ref, ...), custom_call_target="tpu_custom_call" | custom-call | flops 268435456 | bytes 1474560 | tf_op jit(solution)/shard_map/fourier/pallas_call | solution.py:74
  38.4 0.5 gram.5
  38.9 1.7 %gram.6 = (f32[64,128]{1,0:T(8,128)S(1)}, bf16[256,6144]{1,0:T(8,128)(2,1)S(1)}) custom-call(s32[1]{0:T(128)} %bitcast.me_ref, f32[1,6144]{1,0:T(1,128)S(1)} %bitcast.19, bf16[72,1536]{1,0:T(8,128)(2,1)S(1)} %get-tuple-element.47.refs_0_, bf16[72,1536]{1,0:T(8,128)(2,1)S(1)} %collective-permute-done.9.refs_1_, ...), custom_call_target="tpu_custom_call", output_to_operand_aliasing={{1}: (7, {})} | custom-call | flops 402653184 | bytes 1671168 | tf_op jit(solution)/shard_map/gram/pallas_call | solution.py:154
  40.6 10.8 %collective-permute-done.6.refs_1_ = bf16[72,2048]{1,0:T(8,128)(2,1)S(1)} collective-permute-done((bf16[72,2048]{1,0:T(8,128)(2,1)S(1)}, bf16[72,2048]{1,0:T(8,128)(2,1)S(1)}, u32[]{:S(2)}, u32[]{:S(2)}) %collective-permute-start.6) | collective-permute-done | bytes 294944 | tf_op jit(solution)/shard_map/ppermute | solution.py:321
  51.4 0.0 collective-permute-start
  51.4 0.0 collective-permute-done.7.refs_2_
  51.4 0.9 collective-permute-start.1
  52.3 0.0 collective-permute-done.8.refs_3_
  52.3 2.4 %collective-permute-start.2 = (bf16[72,512]{1,0:T(8,128)(2,1)S(1)}, bf16[72,512]{1,0:T(8,128)(2,1)S(1)}, u32[]{:S(2)}, u32[]{:S(2)}) collective-permute-start(bf16[72,512]{1,0:T(8,128)(2,1)S(1)} %get-tuple-element.38), channel_id=1, source_target_pairs={{0,96},{32,0},{64,32},{96,64},{1,97},{33,1},{65,33},{97,65},{2,98}... | collective-permute-start | bytes 221192 | tf_op jit(solution)/shard_map/ppermute | solution.py:321
  54.7 2.1 %gram.7 = (f32[64,128]{1,0:T(8,128)S(1)}, bf16[256,6144]{1,0:T(8,128)(2,1)S(1)}) custom-call(s32[1]{0:T(128)} %bitcast.me_ref, f32[1,6144]{1,0:T(1,128)S(1)} %bitcast.20, bf16[72,2048]{1,0:T(8,128)(2,1)S(1)} %get-tuple-element.43.refs_0_, bf16[72,2048]{1,0:T(8,128)(2,1)S(1)} %collective-permute-done.6.refs_1_, ...), custom_call_target="tpu_custom_call", output_to_operand_aliasing={{1}: (7, {})} | custom-call | flops 536870912 | bytes 2228224 | tf_op jit(solution)/shard_map/gram/pallas_call | solution.py:154
  56.9 0.0 collective-permute-done.4.refs_2_
  56.9 0.0 collective-permute-done.5.refs_3_
  56.9 1.6 %gram.8 = (f32[64,128]{1,0:T(8,128)S(1)}, bf16[256,6144]{1,0:T(8,128)(2,1)S(1)}) custom-call(s32[1]{0:T(128)} %bitcast.me_ref, f32[1,6144]{1,0:T(1,128)S(1)} %bitcast.21, bf16[72,1536]{1,0:T(8,128)(2,1)S(1)} %get-tuple-element.39.refs_0_, bf16[72,1536]{1,0:T(8,128)(2,1)S(1)} %collective-permute-done.3.refs_1_, ...), custom_call_target="tpu_custom_call", output_to_operand_aliasing={{1}: (7, {})} | custom-call | flops 402653184 | bytes 1671168 | tf_op jit(solution)/shard_map/gram/pallas_call | solution.py:154
  58.5 0.0 collective-permute-done.refs_1_
  58.5 0.0 collective-permute-done.1.refs_2_
  58.6 0.1 collective-permute-done.2.refs_3_
  58.6 0.5 gram.9
  59.2 0.1 collective-permute-start.15
  59.3 1.2 %collective-permute-done.15 = f32[64,128]{1,0:T(8,128)S(1)} collective-permute-done((f32[64,128]{1,0:T(8,128)S(1)}, f32[64,128]{1,0:T(8,128)S(1)}, u32[]{:S(2)}, u32[]{:S(2)}) %collective-permute-start.15) | collective-permute-done | bytes 32800 | tf_op jit(solution)/shard_map/ppermute | solution.py:293
  60.5 1.9 %collective-permute-start.16 = (f32[64,128]{1,0:T(8,128)S(1)}, f32[64,128]{1,0:T(8,128)S(1)}, u32[]{:S(2)}, u32[]{:S(2)}) collective-permute-start(f32[64,128]{1,0:T(8,128)S(1)} %add.52), channel_id=1, source_target_pairs={{0,2},{1,3},{2,4},{3,5},{4,6},{5,7},{6,0},{7,1},{8,10},{9,11},{10,... | collective-permute-start | bytes 98312 | tf_op jit(solution)/shard_map/ppermute | solution.py:293
  62.4 2.2 %collective-permute-start.17 = (f32[64,128]{1,0:T(8,128)S(1)}, f32[64,128]{1,0:T(8,128)S(1)}, u32[]{:S(2)}, u32[]{:S(2)}) collective-permute-start(f32[64,128]{1,0:T(8,128)S(1)} %add.52), channel_id=1, source_target_pairs={{0,6},{1,7},{2,0},{3,1},{4,2},{5,3},{6,4},{7,5},{8,14},{9,15},{10,... | collective-permute-start | bytes 98312 | tf_op jit(solution)/shard_map/ppermute | solution.py:293
  64.6 1.8 %collective-permute-start.18 = (f32[64,128]{1,0:T(8,128)S(1)}, f32[64,128]{1,0:T(8,128)S(1)}, u32[]{:S(2)}, u32[]{:S(2)}) collective-permute-start(f32[64,128]{1,0:T(8,128)S(1)} %add.52), channel_id=1, source_target_pairs={{0,4},{1,5},{2,6},{3,7},{4,0},{5,1},{6,2},{7,3},{8,12},{9,13},{10,... | collective-permute-start | bytes 98312 | tf_op jit(solution)/shard_map/ppermute | solution.py:293
  66.4 0.0 collective-permute-done.16
  66.4 0.0 collective-permute-done.17
  66.4 3.6 %collective-permute-done.18 = f32[64,128]{1,0:T(8,128)S(1)} collective-permute-done((f32[64,128]{1,0:T(8,128)S(1)}, f32[64,128]{1,0:T(8,128)S(1)}, u32[]{:S(2)}, u32[]{:S(2)}) %collective-permute-start.18) | collective-permute-done | bytes 32800 | tf_op jit(solution)/shard_map/ppermute | solution.py:293
  70.0 1.6 %collective-permute-start.19 = (f32[64,128]{1,0:T(8,128)S(1)}, f32[64,128]{1,0:T(8,128)S(1)}, u32[]{:S(2)}, u32[]{:S(2)}) collective-permute-start(f32[64,128]{1,0:T(8,128)S(1)} %add_add_fusion.1), channel_id=1, source_target_pairs={{0,8},{1,9},{2,10},{3,11},{4,12},{5,13},{6,14},{7,15},{8,16},{9,17... | collective-permute-start | bytes 98312 | tf_op jit(solution)/shard_map/ppermute | solution.py:293
  71.7 1.7 %collective-permute-start.20 = (f32[64,128]{1,0:T(8,128)S(1)}, f32[64,128]{1,0:T(8,128)S(1)}, u32[]{:S(2)}, u32[]{:S(2)}) collective-permute-start(f32[64,128]{1,0:T(8,128)S(1)} %add_add_fusion.1), channel_id=1, source_target_pairs={{0,24},{1,25},{2,26},{3,27},{4,28},{5,29},{6,30},{7,31},{8,0},{9,1... | collective-permute-start | bytes 98312 | tf_op jit(solution)/shard_map/ppermute | solution.py:293
  73.3 2.0 %collective-permute-start.21 = (f32[64,128]{1,0:T(8,128)S(1)}, f32[64,128]{1,0:T(8,128)S(1)}, u32[]{:S(2)}, u32[]{:S(2)}) collective-permute-start(f32[64,128]{1,0:T(8,128)S(1)} %add_add_fusion.1), channel_id=1, source_target_pairs={{0,16},{1,17},{2,18},{3,19},{4,20},{5,21},{6,22},{7,23},{8,24},{9,... | collective-permute-start | bytes 98312 | tf_op jit(solution)/shard_map/ppermute | solution.py:293
  75.3 0.0 collective-permute-done.19
  75.3 0.3 collective-permute-done.20
  75.6 3.2 %collective-permute-done.21 = f32[64,128]{1,0:T(8,128)S(1)} collective-permute-done((f32[64,128]{1,0:T(8,128)S(1)}, f32[64,128]{1,0:T(8,128)S(1)}, u32[]{:S(2)}, u32[]{:S(2)}) %collective-permute-start.21) | collective-permute-done | bytes 32800 | tf_op jit(solution)/shard_map/ppermute | solution.py:293
  78.8 8.4 %recon.1 = bf16[4,2,3,32,2048]{4,3,2,1,0:T(8,128)(2,1)} custom-call(f32[64,128]{1,0:T(8,128)S(1)} %add_add_fusion.total_ref, bf16[256,6144]{1,0:T(8,128)(2,1)S(1)} %get-tuple-element.64.side_ref), custom_call_target="tpu_custom_call" | custom-call | tf_op jit(solution)/shard_map/recon/pallas_call | solution.py:265
  (14 shorter events, 0.2 us)
Async XLA Ops:
  1.7 1.4 %copy-start = (bf16[128,3,2048]{2,0,1:T(8,128)(2,1)S(1)}, bf16[128,3,2048]{2,0,1:T(8,128)(2,1)}, u32[]{:S(2)}) copy-start(bf16[128,3,2048]{2,0,1:T(8,128)(2,1)} %param.5) | copy-start | bytes 4718596
  6.8 22.2 %collective-permute-start.10 = (bf16[72,1536]{1,0:T(8,128)(2,1)S(1)}, bf16[72,1536]{1,0:T(8,128)(2,1)S(1)}, u32[]{:S(2)}, u32[]{:S(2)}) collective-permute-start(bf16[72,1536]{1,0:T(8,128)(2,1)S(1)} %get-tuple-element.49), channel_id=1, source_target_pairs={{0,64},{32,96},{64,0},{96,32},{1,65},{33,97},{65,1},{97,33},{2,66}... | collective-permute-start | bytes 663560 | tf_op jit(solution)/shard_map/ppermute | solution.py:321
  10.1 21.8 %collective-permute-start.11 = (bf16[72,1536]{1,0:T(8,128)(2,1)S(1)}, bf16[72,1536]{1,0:T(8,128)(2,1)S(1)}, u32[]{:S(2)}, u32[]{:S(2)}) collective-permute-start(bf16[72,1536]{1,0:T(8,128)(2,1)S(1)} %get-tuple-element.50), channel_id=1, source_target_pairs={{0,96},{32,0},{64,32},{96,64},{1,97},{33,1},{65,33},{97,65},{2,98}... | collective-permute-start | bytes 663560 | tf_op jit(solution)/shard_map/ppermute | solution.py:321
  13.0 7.9 %collective-permute-start.12 = (bf16[72,512]{1,0:T(8,128)(2,1)S(1)}, bf16[72,512]{1,0:T(8,128)(2,1)S(1)}, u32[]{:S(2)}, u32[]{:S(2)}) collective-permute-start(bf16[72,512]{1,0:T(8,128)(2,1)S(1)} %get-tuple-element.52), channel_id=1, source_target_pairs={{0,32},{32,64},{64,96},{96,0},{1,33},{33,65},{65,97},{97,1},{2,34}... | collective-permute-start | bytes 221192 | tf_op jit(solution)/shard_map/ppermute | solution.py:321
  13.9 7.1 %collective-permute-start.13 = (bf16[72,512]{1,0:T(8,128)(2,1)S(1)}, bf16[72,512]{1,0:T(8,128)(2,1)S(1)}, u32[]{:S(2)}, u32[]{:S(2)}) collective-permute-start(bf16[72,512]{1,0:T(8,128)(2,1)S(1)} %get-tuple-element.53), channel_id=1, source_target_pairs={{0,64},{32,96},{64,0},{96,32},{1,65},{33,97},{65,1},{97,33},{2,66}... | collective-permute-start | bytes 221192 | tf_op jit(solution)/shard_map/ppermute | solution.py:321
  14.6 14.3 %collective-permute-start.14 = (bf16[72,512]{1,0:T(8,128)(2,1)S(1)}, bf16[72,512]{1,0:T(8,128)(2,1)S(1)}, u32[]{:S(2)}, u32[]{:S(2)}) collective-permute-start(bf16[72,512]{1,0:T(8,128)(2,1)S(1)} %get-tuple-element.54), channel_id=1, source_target_pairs={{0,96},{32,0},{64,32},{96,64},{1,97},{33,1},{65,33},{97,65},{2,98}... | collective-permute-start | bytes 221192 | tf_op jit(solution)/shard_map/ppermute | solution.py:321
  20.9 13.5 %collective-permute-start.9 = (bf16[72,1536]{1,0:T(8,128)(2,1)S(1)}, bf16[72,1536]{1,0:T(8,128)(2,1)S(1)}, u32[]{:S(2)}, u32[]{:S(2)}) collective-permute-start(bf16[72,1536]{1,0:T(8,128)(2,1)S(1)} %get-tuple-element.48), channel_id=1, source_target_pairs={{0,32},{32,64},{64,96},{96,0},{1,33},{33,65},{65,97},{97,1},{2,34}... | collective-permute-start | bytes 663560 | tf_op jit(solution)/shard_map/ppermute | solution.py:321
  21.0 15.6 %copy-start.1 = (f32[3,2048]{1,0:T(4,128)S(1)}, f32[3,2048]{1,0:T(4,128)}, u32[]{:S(2)}) copy-start(f32[3,2048]{1,0:T(4,128)} %param.6) | copy-start | bytes 73732
  21.0 14.2 %collective-permute-start.3 = (bf16[72,1536]{1,0:T(8,128)(2,1)S(1)}, bf16[72,1536]{1,0:T(8,128)(2,1)S(1)}, u32[]{:S(2)}, u32[]{:S(2)}) collective-permute-start(bf16[72,1536]{1,0:T(8,128)(2,1)S(1)} %get-tuple-element.40), channel_id=1, source_target_pairs={{0,32},{32,64},{64,96},{96,0},{1,33},{33,65},{65,97},{97,1},{2,34}... | collective-permute-start | bytes 663560 | tf_op jit(solution)/shard_map/ppermute | solution.py:321
  28.9 22.5 %collective-permute-start.6 = (bf16[72,2048]{1,0:T(8,128)(2,1)S(1)}, bf16[72,2048]{1,0:T(8,128)(2,1)S(1)}, u32[]{:S(2)}, u32[]{:S(2)}) collective-permute-start(bf16[72,2048]{1,0:T(8,128)(2,1)S(1)} %get-tuple-element.44), channel_id=1, source_target_pairs={{0,32},{32,64},{64,96},{96,0},{1,33},{33,65},{65,97},{97,1},{2,34}... | collective-permute-start | bytes 884744 | tf_op jit(solution)/shard_map/ppermute | solution.py:321
  29.1 22.4 %collective-permute-start.7 = (bf16[72,2048]{1,0:T(8,128)(2,1)S(1)}, bf16[72,2048]{1,0:T(8,128)(2,1)S(1)}, u32[]{:S(2)}, u32[]{:S(2)}) collective-permute-start(bf16[72,2048]{1,0:T(8,128)(2,1)S(1)} %get-tuple-element.45), channel_id=1, source_target_pairs={{0,64},{32,96},{64,0},{96,32},{1,65},{33,97},{65,1},{97,33},{2,66}... | collective-permute-start | bytes 884744 | tf_op jit(solution)/shard_map/ppermute | solution.py:321
  31.9 20.4 %collective-permute-start.8 = (bf16[72,2048]{1,0:T(8,128)(2,1)S(1)}, bf16[72,2048]{1,0:T(8,128)(2,1)S(1)}, u32[]{:S(2)}, u32[]{:S(2)}) collective-permute-start(bf16[72,2048]{1,0:T(8,128)(2,1)S(1)} %get-tuple-element.46), channel_id=1, source_target_pairs={{0,96},{32,0},{64,32},{96,64},{1,97},{33,1},{65,33},{97,65},{2,98}... | collective-permute-start | bytes 884744 | tf_op jit(solution)/shard_map/ppermute | solution.py:321
  34.4 22.4 %collective-permute-start.4 = (bf16[72,1536]{1,0:T(8,128)(2,1)S(1)}, bf16[72,1536]{1,0:T(8,128)(2,1)S(1)}, u32[]{:S(2)}, u32[]{:S(2)}) collective-permute-start(bf16[72,1536]{1,0:T(8,128)(2,1)S(1)} %get-tuple-element.41), channel_id=1, source_target_pairs={{0,64},{32,96},{64,0},{96,32},{1,65},{33,97},{65,1},{97,33},{2,66}... | collective-permute-start | bytes 663560 | tf_op jit(solution)/shard_map/ppermute | solution.py:321
  35.2 21.7 %collective-permute-start.5 = (bf16[72,1536]{1,0:T(8,128)(2,1)S(1)}, bf16[72,1536]{1,0:T(8,128)(2,1)S(1)}, u32[]{:S(2)}, u32[]{:S(2)}) collective-permute-start(bf16[72,1536]{1,0:T(8,128)(2,1)S(1)} %get-tuple-element.42), channel_id=1, source_target_pairs={{0,96},{32,0},{64,32},{96,64},{1,97},{33,1},{65,33},{97,65},{2,98}... | collective-permute-start | bytes 663560 | tf_op jit(solution)/shard_map/ppermute | solution.py:321
  51.4 7.1 %collective-permute-start = (bf16[72,512]{1,0:T(8,128)(2,1)S(1)}, bf16[72,512]{1,0:T(8,128)(2,1)S(1)}, u32[]{:S(2)}, u32[]{:S(2)}) collective-permute-start(bf16[72,512]{1,0:T(8,128)(2,1)S(1)} %get-tuple-element.36), channel_id=1, source_target_pairs={{0,32},{32,64},{64,96},{96,0},{1,33},{33,65},{65,97},{97,1},{2,34}... | collective-permute-start | bytes 221192 | tf_op jit(solution)/shard_map/ppermute | solution.py:321
  51.4 7.1 %collective-permute-start.1 = (bf16[72,512]{1,0:T(8,128)(2,1)S(1)}, bf16[72,512]{1,0:T(8,128)(2,1)S(1)}, u32[]{:S(2)}, u32[]{:S(2)}) collective-permute-start(bf16[72,512]{1,0:T(8,128)(2,1)S(1)} %get-tuple-element.37), channel_id=1, source_target_pairs={{0,64},{32,96},{64,0},{96,32},{1,65},{33,97},{65,1},{97,33},{2,66}... | collective-permute-start | bytes 221192 | tf_op jit(solution)/shard_map/ppermute | solution.py:321
  52.3 6.3 %collective-permute-start.2 = (bf16[72,512]{1,0:T(8,128)(2,1)S(1)}, bf16[72,512]{1,0:T(8,128)(2,1)S(1)}, u32[]{:S(2)}, u32[]{:S(2)}) collective-permute-start(bf16[72,512]{1,0:T(8,128)(2,1)S(1)} %get-tuple-element.38), channel_id=1, source_target_pairs={{0,96},{32,0},{64,32},{96,64},{1,97},{33,1},{65,33},{97,65},{2,98}... | collective-permute-start | bytes 221192 | tf_op jit(solution)/shard_map/ppermute | solution.py:321
  59.2 1.3 %collective-permute-start.15 = (f32[64,128]{1,0:T(8,128)S(1)}, f32[64,128]{1,0:T(8,128)S(1)}, u32[]{:S(2)}, u32[]{:S(2)}) collective-permute-start(f32[64,128]{1,0:T(8,128)S(1)} %get-tuple-element.63), channel_id=1, source_target_pairs={{0,1},{1,0},{2,3},{3,2},{4,5},{5,4},{6,7},{7,6},{8,9},{9,8},{10,11... | collective-permute-start | bytes 98312 | tf_op jit(solution)/shard_map/ppermute | solution.py:293
  60.5 5.9 %collective-permute-start.16 = (f32[64,128]{1,0:T(8,128)S(1)}, f32[64,128]{1,0:T(8,128)S(1)}, u32[]{:S(2)}, u32[]{:S(2)}) collective-permute-start(f32[64,128]{1,0:T(8,128)S(1)} %add.52), channel_id=1, source_target_pairs={{0,2},{1,3},{2,4},{3,5},{4,6},{5,7},{6,0},{7,1},{8,10},{9,11},{10,... | collective-permute-start | bytes 98312 | tf_op jit(solution)/shard_map/ppermute | solution.py:293
  62.4 4.0 %collective-permute-start.17 = (f32[64,128]{1,0:T(8,128)S(1)}, f32[64,128]{1,0:T(8,128)S(1)}, u32[]{:S(2)}, u32[]{:S(2)}) collective-permute-start(f32[64,128]{1,0:T(8,128)S(1)} %add.52), channel_id=1, source_target_pairs={{0,6},{1,7},{2,0},{3,1},{4,2},{5,3},{6,4},{7,5},{8,14},{9,15},{10,... | collective-permute-start | bytes 98312 | tf_op jit(solution)/shard_map/ppermute | solution.py:293
  64.6 5.4 %collective-permute-start.18 = (f32[64,128]{1,0:T(8,128)S(1)}, f32[64,128]{1,0:T(8,128)S(1)}, u32[]{:S(2)}, u32[]{:S(2)}) collective-permute-start(f32[64,128]{1,0:T(8,128)S(1)} %add.52), channel_id=1, source_target_pairs={{0,4},{1,5},{2,6},{3,7},{4,0},{5,1},{6,2},{7,3},{8,12},{9,13},{10,... | collective-permute-start | bytes 98312 | tf_op jit(solution)/shard_map/ppermute | solution.py:293
  70.0 5.3 %collective-permute-start.19 = (f32[64,128]{1,0:T(8,128)S(1)}, f32[64,128]{1,0:T(8,128)S(1)}, u32[]{:S(2)}, u32[]{:S(2)}) collective-permute-start(f32[64,128]{1,0:T(8,128)S(1)} %add_add_fusion.1), channel_id=1, source_target_pairs={{0,8},{1,9},{2,10},{3,11},{4,12},{5,13},{6,14},{7,15},{8,16},{9,17... | collective-permute-start | bytes 98312 | tf_op jit(solution)/shard_map/ppermute | solution.py:293
  71.7 3.9 %collective-permute-start.20 = (f32[64,128]{1,0:T(8,128)S(1)}, f32[64,128]{1,0:T(8,128)S(1)}, u32[]{:S(2)}, u32[]{:S(2)}) collective-permute-start(f32[64,128]{1,0:T(8,128)S(1)} %add_add_fusion.1), channel_id=1, source_target_pairs={{0,24},{1,25},{2,26},{3,27},{4,28},{5,29},{6,30},{7,31},{8,0},{9,1... | collective-permute-start | bytes 98312 | tf_op jit(solution)/shard_map/ppermute | solution.py:293
  73.3 5.4 %collective-permute-start.21 = (f32[64,128]{1,0:T(8,128)S(1)}, f32[64,128]{1,0:T(8,128)S(1)}, u32[]{:S(2)}, u32[]{:S(2)}) collective-permute-start(f32[64,128]{1,0:T(8,128)S(1)} %add_add_fusion.1), channel_id=1, source_target_pairs={{0,16},{1,17},{2,18},{3,19},{4,20},{5,21},{6,22},{7,23},{8,24},{9,... | collective-permute-start | bytes 98312 | tf_op jit(solution)/shard_map/ppermute | solution.py:293

commit v2 on v0

v2 whole, which is shorter than its diff:
```python
import functools
import math

import jax
import jax.numpy as jnp
from jax import lax
from jax.experimental import pallas as pl
from jax.experimental.pallas import tpu as pltpu
from jax.sharding import PartitionSpec as P

MODES = 4
EIG_ITERS = 3
TILE = 512
CHUNKS = (2048, 2048, 1536, 512)
COST = 1000000


def pieces(start, width, points, most):
    result = []
    at = 0
    while at < width:
        column = (start + at) % points
        size = min(most, width - at, points - column)
        result.append((at, (start + at) // points, column, size))
        at += size
    return result


def band_kernel(me_ref, freq_ref, x_ref, tail_ref, *refs, parts):
    outs, refs = refs[:4], refs[4:]
    band_ref, edge_ref, freqs, table_ref, freq_sem = refs[:5]
    fetches = start_fetches(me_ref, x_ref, tail_ref, refs[5:], parts)
    fetch = pltpu.make_async_copy(freq_ref, freqs, freq_sem)
    fetch.start()
    fetch.wait()
    me = me_ref[0]
    half = edge_ref.shape[1]
    length = 2 * half
    row = lax.broadcasted_iota(jnp.int32, (32, length), 0)
    steps = lax.broadcasted_iota(jnp.int32, (32, length), 1)
    bins = jnp.zeros((32, length), jnp.int32)
    for k in range(16):
        bins = jnp.where(row // 2 == k, freqs[lax.rem(4 * me + k, 16)], bins)
    turns = (bins * steps + (length // 4) * lax.rem(row, 2)) & (length - 1)
    window = 0.5 - 0.5 * jnp.cos(steps[:1].astype(jnp.float32) * (2.0 * math.pi / length))
    table = window * jnp.cos(turns.astype(jnp.float32) * (2.0 * math.pi / length))
    table_ref[...] = table
    edge_ref[...] = table[:, half:].astype(jnp.bfloat16)
    block = lax.broadcasted_iota(jnp.int32, (8, half), 0)
    for r in range(0, 32, 2):
        for part in range(8):
            rows = []
            for one in (r, r + 1):
                value = jnp.where(block == part, table_ref[one : one + 1, :half], 0.0)
                rows.append(jnp.where(block == part - 1, table_ref[one : one + 1, half:], value))
            band_ref[8 * r : 8 * r + 16, half * part : half * part + half] = jnp.concatenate(
                rows, axis=0
            ).astype(jnp.bfloat16)
    transform(me_ref, band_ref, edge_ref, outs, refs[5:], parts, fetches)


def fourier_kernel(me_ref, band_ref, edge_ref, x_ref, tail_ref, *refs, parts):
    outs, refs = refs[:4], refs[4:]
    fetches = start_fetches(me_ref, x_ref, tail_ref, refs[1:], parts)
    refs[0][0] = me_ref[0]
    transform(me_ref, band_ref, edge_ref, outs, refs[1:], parts, fetches)


def start_fetches(me_ref, x_ref, tail_ref, scratch, parts):
    held, tails, sems, tail_sems = scratch
    fetches = []
    for k, (at, comp, column, size) in enumerate(parts):
        source, here = pl.ds(column, size), pl.ds(at, size)
        fetches.append(
            (
                pltpu.make_async_copy(x_ref.at[comp, :, source], held.at[:, here], sems.at[k]),
                pltpu.make_async_copy(
                    tail_ref.at[comp, :, source], tails.at[:, here], tail_sems.at[k]
                ),
            )
        )
    for fetch, _ in fetches:
        fetch.start()

    @pl.when(me_ref[0] == 0)
    def _():
        for _, fetch_tail in fetches:
            fetch_tail.start()

    return fetches


def transform(me_ref, band_ref, edge_ref, outs, scratch, parts, fetches):
    held, tails = scratch[:2]
    half = tails.shape[0]

    def edge(rows, here):
        result = jnp.dot(edge_ref[...], rows, preferred_element_type=jnp.float32)
        result = result.astype(jnp.bfloat16)
        for peer, out in enumerate(outs):
            out[64:, here] = result[8 * peer : 8 * peer + 8]

    for (at, _, _, size), (fetch, fetch_tail) in zip(parts, fetches):
        here = slice(at, at + size)
        fetch.wait()
        main = jnp.dot(band_ref[...], held[:, here], preferred_element_type=jnp.float32)
        main = main.astype(jnp.bfloat16)
        for peer, out in enumerate(outs):
            out[:64, here] = main[64 * peer : 64 * peer + 64]

        @pl.when(me_ref[0] == 0)
        def _():
            fetch_tail.wait()
            edge(tails[:, here], here)

        @pl.when(me_ref[0] != 0)
        def _():
            edge(held[:half, here], here)


def fourier(me, freq_bins, band, edge, snapshots, tail, start, width):
    comps, rows, points = snapshots.shape
    half = tail.shape[1]
    parts = pieces(start, width, points, TILE)
    vmem = pl.BlockSpec(memory_space=pltpu.VMEM)
    smem = pl.BlockSpec(memory_space=pltpu.SMEM)
    hbm = pl.BlockSpec(memory_space=pl.ANY)
    out_shape = [jax.ShapeDtypeStruct((72, width), jnp.bfloat16)] * 4
    scratch = [
        pltpu.VMEM((rows, width), jnp.bfloat16),
        pltpu.VMEM((half, width), jnp.bfloat16),
        pltpu.SemaphoreType.DMA((len(parts),)),
        pltpu.SemaphoreType.DMA((len(parts),)),
    ]
    if band is None:
        kernel, operands, in_specs = band_kernel, (me, freq_bins), [smem, hbm]
        out_shape = out_shape + [
            jax.ShapeDtypeStruct((256, rows), jnp.bfloat16),
            jax.ShapeDtypeStruct((32, half), jnp.bfloat16),
        ]
        out_specs = [vmem] * 6
        scratch = [
            pltpu.SMEM(freq_bins.shape, jnp.int32),
            pltpu.VMEM((32, 2 * half), jnp.float32),
            pltpu.SemaphoreType.DMA,
        ] + scratch
    else:
        kernel, operands, in_specs = fourier_kernel, (me, band, edge), [smem, vmem, vmem]
        out_shape = out_shape + [jax.ShapeDtypeStruct((1,), jnp.int32)]
        out_specs = [vmem] * 4 + [smem]
    return pl.pallas_call(
        functools.partial(kernel, parts=parts),
        in_specs=in_specs + [hbm] * 2,
        out_specs=out_specs,
        out_shape=out_shape,
        scratch_shapes=scratch,
        compiler_params=pltpu.CompilerParams(vmem_limit_bytes=48 * 2**20),
        cost_estimate=pl.CostEstimate(
            flops=COST * width, bytes_accessed=COST * width, transcendentals=0
        ),
        name="fourier",
    )(*operands, snapshots, tail)


def gram_kernel(me_ref, weight_ref, *refs, runs):
    parts, refs = refs[:4], refs[4:]
    total_in = refs[0] if len(refs) == 4 else None
    total_ref, side_ref, total = refs[-3:]
    me = me_ref[0]
    for at, comp, column, size in runs:
        here = slice(at, at + size)
        last = lax.broadcasted_iota(jnp.int32, (8, size), 0) == 7
        weight = weight_ref[comp : comp + 1, column : column + size]
        for peer in range(4):
            group = lax.rem(me - peer + 4, 4)
            rows = parts[peer][:64, here].astype(jnp.float32)
            edge = parts[(peer - 1) % 4][64:72, here].astype(jnp.float32)
            blocks = [
                rows[8 * k : 8 * k + 8] + jnp.where(last, edge[k : k + 1], 0.0) for k in range(8)
            ]
            for freq in range(4):
                both = jnp.concatenate(blocks[2 * freq : 2 * freq + 2], axis=0)
                start = pl.multiple_of(64 * freq + 16 * group, 16)
                side_ref[pl.ds(start, 16), here] = both.astype(jnp.bfloat16)
        side = side_ref[:, here]
        scaled = side.astype(jnp.float32) * weight
        high = scaled.astype(jnp.bfloat16)
        low = (scaled - high.astype(jnp.float32)).astype(jnp.bfloat16)
        dims = (((1,), (1,)), ((), ()))
        added = lax.dot_general(
            high, side, dims, preferred_element_type=jnp.float32
        ) + lax.dot_general(low, side, dims, preferred_element_type=jnp.float32)
        total[...] = added if at == 0 else total[...] + added
    lane = lax.broadcasted_iota(jnp.int32, (8, 128), 1)
    real_lane = lax.rem(lane, 16) < 8
    low_lane = lane < 64
    for pair in range(2):
        for group in range(4):
            tops = []
            for freq in (2 * pair, 2 * pair + 1):
                start = 64 * freq + 16 * group
                columns = slice(128 * pair, 128 * pair + 128)
                real = total[start : start + 8, columns]
                imag = total[start + 8 : start + 16, columns]
                turned = jnp.where(real_lane, pltpu.roll(imag, 120, 1), -pltpu.roll(imag, 8, 1))
                tops.append(real + turned)
            rows = slice(32 * pair + 8 * group, 32 * pair + 8 * group + 8)
            top = jnp.where(low_lane, tops[0], tops[1])
            total_ref[rows, :] = top if total_in is None else top + total_in[rows, :]


def gram(me, weight, parts, before, start, width):
    vmem = pl.BlockSpec(memory_space=pltpu.VMEM)
    return pl.pallas_call(
        functools.partial(gram_kernel, runs=pieces(start, width, weight.shape[1], TILE)),
        in_specs=[pl.BlockSpec(memory_space=pltpu.SMEM)] + [vmem] * (5 + len(before)),
        out_specs=[vmem] * 2,
        out_shape=[
            jax.ShapeDtypeStruct((64, 128), jnp.float32),
            jax.ShapeDtypeStruct((256, width), jnp.bfloat16),
        ],
        scratch_shapes=[pltpu.VMEM((256, 256), jnp.float32)],
        compiler_params=pltpu.CompilerParams(vmem_limit_bytes=32 * 2**20),
        cost_estimate=pl.CostEstimate(
            flops=COST * width, bytes_accessed=COST * width, transcendentals=0
        ),
        name="gram",
    )(me, weight, *parts, *before)


def split(value):
    high = value.astype(jnp.bfloat16).astype(jnp.float32)
    rest = value - high
    mid = rest.astype(jnp.bfloat16).astype(jnp.float32)
    return high, mid, rest - mid


def projections(total_ref, proj_ref):
    shape = (2, 8, 128)
    lane = lax.broadcasted_iota(jnp.int32, shape, 2)
    row = lax.broadcasted_iota(jnp.int32, shape, 1)
    real_lane = lax.rem(lane, 16) < 8
    low_lane = lane < 64
    low_row = row < 4
    place = lax.rem(row, 4)

    def turn(value):
        return jnp.where(real_lane, -pltpu.roll(value, 120, 2), pltpu.roll(value, 8, 2))

    def pick(value, j):
        return jnp.where(low_row, value[:, j : j + 1], value[:, 4 + j : 5 + j])

    def orthonormal(base):
        other = turn(base)
        for j in range(MODES):
            one, two = pick(base, j), pick(other, j)
            along = jnp.sum(base * one, axis=2, keepdims=True)
            across = jnp.sum(base * two, axis=2, keepdims=True)
            scale = lax.rsqrt(pick(along, j))
            a, b = along * scale * scale, across * scale * scale
            later = place > j
            new_base = jnp.where(later, base - a * one - b * two, base)
            new_other = jnp.where(later, other - a * two + b * one, other)
            here = place == j
            base = jnp.where(here, base * scale, new_base)
            other = jnp.where(here, other * scale, new_other)
        return base, other

    def wide(left, right):
        return jnp.concatenate([left, right], axis=1)

    groups = [
        jnp.stack([total_ref[32 * pair + 8 * g : 32 * pair + 8 * g + 8, :] for pair in range(2)])
        for g in range(4)
    ]
    rows = []
    for keep in (low_lane, jnp.logical_not(low_lane)):
        for group in groups:
            top = jnp.where(keep, group, 0.0)
            rows += [top, turn(top)]
    operators = []
    for pair in range(2):
        high, mid, low = split(jnp.concatenate([value[pair] for value in rows], axis=0))
        operators.append(
            jnp.concatenate([wide(high, low), wide(mid, jnp.zeros_like(mid))], axis=0).astype(
                jnp.bfloat16
            )
        )
    first = groups[0]
    base = jnp.where(low_row, first, pltpu.roll(first, 4, 1))
    base = jnp.where(low_row == low_lane, base, 0.0)
    base, other = orthonormal(base)
    for sweep in range(EIG_ITERS):
        high, mid, low = split(base)
        zero = jnp.zeros_like(low[0])
        results = []
        for pair in range(2):
            terms = jnp.concatenate(
                [
                    wide(high[pair], high[pair]),
                    wide(mid[pair], mid[pair]),
                    wide(low[pair], zero),
                    wide(zero, zero),
                ],
                axis=0,
            ).astype(jnp.bfloat16)
            results.append(jnp.dot(terms, operators[pair], preferred_element_type=jnp.float32))
        base = jnp.stack(
            [
                terms[:8, :128] + (terms[:8, 128:] + terms[8:16, :128] + terms[16:24, :128])
                for terms in results
            ]
        )
        base, other = orthonormal(base)
    high, mid, low = split(jnp.concatenate([base, other], axis=1))
    for pair in range(2):
        whole = lax.dot_general(
            jnp.concatenate([high[pair], high[pair], mid[pair]], axis=0).astype(jnp.bfloat16),
            jnp.concatenate([high[pair], mid[pair], high[pair]], axis=0).astype(jnp.bfloat16),
            (((0,), (0,)), ((), ())),
            preferred_element_type=jnp.float32,
        )
        ordered = []
        for freq in range(2):
            for part in range(2):
                for group in range(4):
                    start = 64 * freq + 16 * group + 8 * part
                    ordered.append(whole[start : start + 8])
        proj_ref[pair] = jnp.concatenate(ordered, axis=0).astype(jnp.bfloat16)


def recon_kernel(total_ref, *refs, runs):
    sides, (out_ref, proj_ref, held, sems) = refs[:-4], refs[-4:]
    projections(total_ref, proj_ref)
    sends = []
    for k, (side, at, comp, column, size) in enumerate(runs):
        for pair in range(2):
            result = jnp.dot(
                proj_ref[pair],
                sides[side][128 * pair : 128 * pair + 128, at : at + size],
                preferred_element_type=jnp.float32,
            ).astype(jnp.bfloat16)
            for freq in range(2):
                for part in range(2):
                    start = 64 * freq + 32 * part
                    held[2 * pair + freq, part, comp, :, column : column + size] = result[
                        start : start + 32
                    ]
        columns = pl.ds(column, size)
        send = pltpu.make_async_copy(
            held.at[:, :, comp, :, columns], out_ref.at[:, :, comp, :, columns], sems.at[k]
        )
        send.start()
        sends.append(send)
    for send in sends:
        send.wait()


def recon(total, sides, comps, points):
    runs = []
    start = 0
    for k, side in enumerate(sides):
        width = side.shape[1]
        runs += [(k, *piece) for piece in pieces(start, width, points, 2 * TILE)]
        start += width
    shape = (4, 2, comps, 32, points)
    return pl.pallas_call(
        functools.partial(recon_kernel, runs=runs),
        in_specs=[pl.BlockSpec(memory_space=pltpu.VMEM)] * (1 + len(sides)),
        out_specs=pl.BlockSpec(memory_space=pl.ANY),
        out_shape=jax.ShapeDtypeStruct(shape, jnp.bfloat16),
        scratch_shapes=[
            pltpu.VMEM((2, 128, 128), jnp.bfloat16),
            pltpu.VMEM(shape, jnp.bfloat16),
            pltpu.SemaphoreType.DMA((len(runs),)),
        ],
        compiler_params=pltpu.CompilerParams(vmem_limit_bytes=32 * 2**20),
        name="recon",
    )(total, *sides)


def point_sum(value):
    def index(y, z, core):
        return y * 8 + z * 2 + core

    partners = (
        lambda y, z, core: (y, z, 1 - core),
        lambda y, z, core: (y, z ^ 1, 1 - core),
        lambda y, z, core: (y, 3 - z, 1 - core),
        lambda y, z, core: (y ^ 1, z, 1 - core),
        lambda y, z, core: (3 - y, z, 1 - core),
    )
    for partner in partners:
        pairs = [
            (index(y, z, core), index(*partner(y, z, core)))
            for y in range(4)
            for z in range(4)
            for core in range(2)
        ]
        value = value + lax.ppermute(value, "pts", pairs)
    return value


def on_device(snapshots, tail_rows, point_weight, freq_bins):
    _, comps, points = snapshots.shape
    snapshots = jnp.transpose(snapshots, (1, 0, 2))
    tail = jnp.transpose(tail_rows, (1, 0, 2))
    me = lax.axis_index("blk").astype(jnp.int32).reshape(1)
    band = edge = None
    token = me
    arrived = []
    start = 0
    for width in CHUNKS:
        result = fourier(token, freq_bins, band, edge, snapshots, tail, start, width)
        sent = result[:4]
        if band is None:
            band, edge = result[4:]
        else:
            token = result[4]
        parts = [sent[0]]
        for shift in (1, 3, 2):
            pairs = [(k, (k + shift) % 4) for k in range(4)]
            parts.append(lax.ppermute(sent[shift], "blk", pairs))
        arrived.append((start, width, [parts[k] for k in (0, 1, 3, 2)]))
        start += width
    before = ()
    sides = []
    for start, width, parts in arrived:
        total, side = gram(me, point_weight, parts, before, start, width)
        before = (total,)
        sides.append(side)
    out = recon(point_sum(total), sides, comps, points)
    return jnp.transpose(out, (0, 1, 3, 2, 4))


def solution(mesh):
    in_specs = (P("blk", None, "pts"), P(None, None, "pts"), P(None, "pts"), P())
    out_specs = P("blk", None, None, None, "pts")
    return jax.shard_map(
        on_device, mesh=mesh, in_specs=in_specs, out_specs=out_specs, check_vma=False
    )
```

time: 451 us -> 74 us (0.16)
  waiting for transfers between devices: 224 us -> 22.7 us
  local copies, waits for them, and re-layouts: 115 us -> 2.07 us
  other arithmetic: 58 us -> 0.03 us
  matrix products: 36.9 us -> 0 us
  Pallas kernels: 0 us -> 24 us
  starting transfers between devices: 1.5 us -> 24.6 us
  between operations: 13.8 us -> 0.26 us
    all_gather x1 -> x0, waiting for transfers between devices: 122 us -> none  [on_device(): gathered = lax.all_gather(coefficients, 'blk', axis=2, tiled=True)]
    psum x1 -> x0, waiting for transfers between devices: 101 us -> none  [on_device(): lax.psum(weighted_gram(side_rows, weight), 'pts')]
    slice x16 -> x0, local copies, waits for them, and re-layouts: 73.6 us -> none  [the longest x2 53.3 us: on_device(): halves[:-1]]
    another operation x82 -> x0, other arithmetic: 48 us -> none  [the longest x48 22.5 us: orthonormal(): factor = jnp.linalg.cholesky(inner)]
    dot_general x42 -> x0, matrix products: 33.8 us -> none  [the longest x1 9.42 us: on_device(): jnp.einsum('fn,bnq->fbq', table[:, :half_len], halves[:-1], preferred_ele...]
    pallas_call x0 -> x9, Pallas kernels: none -> 24 us  [the longest x4 15.1 us: fourier(): pl.pallas_call(functools.partial(kernel, parts=parts), in_specs=in_specs...]
    ppermute x1 -> x17, starting transfers between devices: 1.28 us -> 24.6 us  [the longest x12 12.8 us: on_device(): parts.append(lax.ppermute(sent[shift], 'blk', pairs))]
    ppermute x1 -> x17, waiting for transfers between devices: 0.01 us -> 22.7 us  [the longest x12 14.9 us: on_device(): parts.append(lax.ppermute(sent[shift], 'blk', pairs))]
  transfers between devices with their start and end apart: 3 -> 17, of which waited for: 2 -> 11; matrix products, arithmetic and copies ran while one was open for 14% -> 0% of each run, Pallas kernels for 0% -> 20%
where the time goes in v2:
time: 74 us; the launch traced here: 73.8 us
  starting transfers between devices  24.6 us (33%)
  Pallas kernels  24 us (32%)
  waiting for transfers between devices  22.7 us (31%)
  local copies, waits for them, and re-layouts  2.07 us (3%)
    pallas_call x4, Pallas kernels, fourier(): pl.pallas_call(functools.partial(kernel, parts=parts), in_specs=in_specs...  15.1 us
    ppermute x12, waiting for transfers between devices, on_device(): parts.append(lax.ppermute(sent[shift], 'blk', pairs))  14.9 us
    ppermute x12, starting transfers between devices, on_device(): parts.append(lax.ppermute(sent[shift], 'blk', pairs))  12.8 us
    ppermute x5, starting transfers between devices, point_sum(): value = value + lax.ppermute(value, 'pts', pairs)  11.8 us
    ppermute x5, waiting for transfers between devices, point_sum(): value = value + lax.ppermute(value, 'pts', pairs)  7.79 us
    pallas_call x1, Pallas kernels, recon(): pl.pallas_call(functools.partial(recon_kernel, runs=runs), in_specs=[pl.B...  4.89 us
    pallas_call x4, Pallas kernels, gram(): pl.pallas_call(functools.partial(gram_kernel, runs=pieces(start, width, w...  4.04 us
    unnamed x8, local copies, waits for them, and re-layouts  2.07 us
  transfers between devices with their start and end apart: 17, of which 11 were waited for; matrix products, arithmetic and copies ran while one was open for 0% of the time, Pallas kernels for 20%

profile of v2, /device:TPU:1, one launch (start us, length us, event | category | flops | bytes accessed | tf_op | source)
XLA Modules:
  0.0 73.8 jit_solution(8612513288052153814)
XLA Ops:
  0.0 0.0 copy-start
  0.0 1.4 %copy-done = bf16[128,3,2048]{2,0,1:T(8,128)(2,1)S(1)} copy-done((bf16[128,3,2048]{2,0,1:T(8,128)(2,1)S(1)}, bf16[128,3,2048]{2,0,1:T(8,128)(2,1)}, u32[]{:S(2)}) %copy-start) | copy-done | bytes 1572888
  1.4 0.0 copy-start.2
  1.4 0.7 copy-done.2
  2.1 0.0 copy-start.1
  2.1 3.7 %fourier.4 = (bf16[72,2048]{1,0:T(8,128)(2,1)S(1)}, bf16[72,2048]{1,0:T(8,128)(2,1)S(1)}, bf16[72,2048]{1,0:T(8,128)(2,1)S(1)}, bf16[72,2048]{1,0:T(8,128)(2,1)S...) custom-call(s32[1]{0:T(128)} %bitcast.me_ref, s32[16]{0:T(128)S(1)} %copy-done.2, ...), custom_call_target="tpu_custom_call" | custom-call | flops 2048000000 | bytes 2048000000 | tf_op jit(solution)/shard_map/fourier/pallas_call | solution.py:151
  5.8 2.1 %collective-permute-start.9 = (bf16[72,2048]{1,0:T(8,128)(2,1)S(1)}, bf16[72,2048]{1,0:T(8,128)(2,1)S(1)}, u32[]{:S(2)}, u32[]{:S(2)}) collective-permute-start(bf16[72,2048]{1,0:T(8,128)(2,1)S(1)} %get-tuple-element.50), channel_id=1, source_target_pairs={{0,32},{32,64},{64,96},{96,0},{1,33},{33,65},{65,97},{97,1},{2,34}... | collective-permute-start | bytes 884744 | tf_op jit(solution)/shard_map/ppermute | solution.py:423
  7.9 2.4 %collective-permute-start.10 = (bf16[72,2048]{1,0:T(8,128)(2,1)S(1)}, bf16[72,2048]{1,0:T(8,128)(2,1)S(1)}, u32[]{:S(2)}, u32[]{:S(2)}) collective-permute-start(bf16[72,2048]{1,0:T(8,128)(2,1)S(1)} %get-tuple-element.51), channel_id=1, source_target_pairs={{0,64},{32,96},{64,0},{96,32},{1,65},{33,97},{65,1},{97,33},{2,66}... | collective-permute-start | bytes 884744 | tf_op jit(solution)/shard_map/ppermute | solution.py:423
  10.4 1.2 %collective-permute-start.11 = (bf16[72,2048]{1,0:T(8,128)(2,1)S(1)}, bf16[72,2048]{1,0:T(8,128)(2,1)S(1)}, u32[]{:S(2)}, u32[]{:S(2)}) collective-permute-start(bf16[72,2048]{1,0:T(8,128)(2,1)S(1)} %get-tuple-element.52), channel_id=1, source_target_pairs={{0,96},{32,0},{64,32},{96,64},{1,97},{33,1},{65,33},{97,65},{2,98}... | collective-permute-start | bytes 884744 | tf_op jit(solution)/shard_map/ppermute | solution.py:423
  11.5 0.0 copy-done.1
  11.5 4.1 %fourier.5 = (bf16[72,2048]{1,0:T(8,128)(2,1)S(1)}, bf16[72,2048]{1,0:T(8,128)(2,1)S(1)}, bf16[72,2048]{1,0:T(8,128)(2,1)S(1)}, bf16[72,2048]{1,0:T(8,128)(2,1)S(1)}, s32[1]{0:T(128)}) custom-call(s32[1]{0:T(128)} %bitcast.me_ref, bf16[256,1024]{1,0:T(8,128)(2,1)S(1)} %get-tuple-element.33.band_ref, bf16[32,128]{1,0:T(8,128)(2,1)S(1)} %get-tuple-element.34.edge_ref, ...), custom_call_target="tpu_custom_call" | custom-call | flops 2048000000 | bytes 2048000000 | tf_op jit(solution)/shard_map/fourier/pallas_call | solution.py:151
  15.7 0.4 collective-permute-start.6
  16.1 0.9 %collective-permute-start.7 = (bf16[72,2048]{1,0:T(8,128)(2,1)S(1)}, bf16[72,2048]{1,0:T(8,128)(2,1)S(1)}, u32[]{:S(2)}, u32[]{:S(2)}) collective-permute-start(bf16[72,2048]{1,0:T(8,128)(2,1)S(1)} %get-tuple-element.47), channel_id=1, source_target_pairs={{0,64},{32,96},{64,0},{96,32},{1,65},{33,97},{65,1},{97,33},{2,66}... | collective-permute-start | bytes 884744 | tf_op jit(solution)/shard_map/ppermute | solution.py:423
  16.9 0.0 collective-permute-done.9.refs_1_
  16.9 1.6 %collective-permute-start.8 = (bf16[72,2048]{1,0:T(8,128)(2,1)S(1)}, bf16[72,2048]{1,0:T(8,128)(2,1)S(1)}, u32[]{:S(2)}, u32[]{:S(2)}) collective-permute-start(bf16[72,2048]{1,0:T(8,128)(2,1)S(1)} %get-tuple-element.48), channel_id=1, source_target_pairs={{0,96},{32,0},{64,32},{96,64},{1,97},{33,1},{65,33},{97,65},{2,98}... | collective-permute-start | bytes 884744 | tf_op jit(solution)/shard_map/ppermute | solution.py:423
  18.6 4.2 %fourier.6 = (bf16[72,1536]{1,0:T(8,128)(2,1)S(1)}, bf16[72,1536]{1,0:T(8,128)(2,1)S(1)}, bf16[72,1536]{1,0:T(8,128)(2,1)S(1)}, bf16[72,1536]{1,0:T(8,128)(2,1)S(1)}, s32[1]{0:T(128)}) custom-call(s32[1]{0:T(128)} %get-tuple-element.35.me_ref, bf16[256,1024]{1,0:T(8,128)(2,1)S(1)} %get-tuple-element.33.band_ref, ...), custom_call_target="tpu_custom_call" | custom-call | flops 1536000000 | bytes 1536000000 | tf_op jit(solution)/shard_map/fourier/pallas_call | solution.py:151
  22.7 0.0 copy-start.3
  22.7 3.0 %fourier.7 = (bf16[72,512]{1,0:T(8,128)(2,1)S(1)}, bf16[72,512]{1,0:T(8,128)(2,1)S(1)}, bf16[72,512]{1,0:T(8,128)(2,1)S(1)}, bf16[72,512]{1,0:T(8,128)(2,1)S(1)}, s32[1]{0:T(128)}) custom-call(s32[1]{0:T(128)} %get-tuple-element.36.me_ref, bf16[256,1024]{1,0:T(8,128)(2,1)S(1)} %get-tuple-element.33.band_ref, bf16[32,128]{1,0:T(8,128)(2,1)S(1)} %get-tuple-element.34.edge_ref, ...), custom_call_target="tpu_custom_call" | custom-call | flops 512000000 | bytes 512000000 | tf_op jit(solution)/shard_map/fourier/pallas_call | solution.py:151
  25.8 0.0 collective-permute-done.10.refs_2_
  25.8 0.5 collective-permute-start.3
  26.3 0.0 collective-permute-done.11.refs_3_
  26.3 1.9 %collective-permute-start.4 = (bf16[72,1536]{1,0:T(8,128)(2,1)S(1)}, bf16[72,1536]{1,0:T(8,128)(2,1)S(1)}, u32[]{:S(2)}, u32[]{:S(2)}) collective-permute-start(bf16[72,1536]{1,0:T(8,128)(2,1)S(1)} %get-tuple-element.43), channel_id=1, source_target_pairs={{0,64},{32,96},{64,0},{96,32},{1,65},{33,97},{65,1},{97,33},{2,66}... | collective-permute-start | bytes 663560 | tf_op jit(solution)/shard_map/ppermute | solution.py:423
  28.2 3.3 %collective-permute-done.6.refs_1_ = bf16[72,2048]{1,0:T(8,128)(2,1)S(1)} collective-permute-done((bf16[72,2048]{1,0:T(8,128)(2,1)S(1)}, bf16[72,2048]{1,0:T(8,128)(2,1)S(1)}, u32[]{:S(2)}, u32[]{:S(2)}) %collective-permute-start.6) | collective-permute-done | bytes 294944 | tf_op jit(solution)/shard_map/ppermute | solution.py:423
  31.5 0.0 collective-permute-start.5
  31.5 0.0 copy-done.3
  31.5 1.3 %gram.4 = (f32[64,128]{1,0:T(8,128)S(1)}, bf16[256,2048]{1,0:T(8,128)(2,1)S(1)}) custom-call(s32[1]{0:T(128)} %bitcast.me_ref, f32[3,2048]{1,0:T(4,128)S(1)} %copy-done.3, bf16[72,2048]{1,0:T(8,128)(2,1)S(1)} %get-tuple-element.49.refs_0_, bf16[72,2048]{1,0:T(8,128)(2,1)S(1)} %collective-permute-done.9.refs_1_, ...), custom_call_target="tpu_custom_call" | custom-call | flops 2048000000 | bytes 2048000000 | tf_op jit(solution)/shard_map/gram/pallas_call | solution.py:214
  32.8 3.1 %collective-permute-done.7.refs_2_ = bf16[72,2048]{1,0:T(8,128)(2,1)S(1)} collective-permute-done((bf16[72,2048]{1,0:T(8,128)(2,1)S(1)}, bf16[72,2048]{1,0:T(8,128)(2,1)S(1)}, u32[]{:S(2)}, u32[]{:S(2)}) %collective-permute-start.7) | collective-permute-done | bytes 294944 | tf_op jit(solution)/shard_map/ppermute | solution.py:423
  35.8 0.0 collective-permute-start
  35.8 0.2 collective-permute-done.8.refs_3_
  36.1 1.8 %collective-permute-start.1 = (bf16[72,512]{1,0:T(8,128)(2,1)S(1)}, bf16[72,512]{1,0:T(8,128)(2,1)S(1)}, u32[]{:S(2)}, u32[]{:S(2)}) collective-permute-start(bf16[72,512]{1,0:T(8,128)(2,1)S(1)} %get-tuple-element.39), channel_id=1, source_target_pairs={{0,64},{32,96},{64,0},{96,32},{1,65},{33,97},{65,1},{97,33},{2,66}... | collective-permute-start | bytes 221192 | tf_op jit(solution)/shard_map/ppermute | solution.py:423
  37.9 1.3 %gram.5 = (f32[64,128]{1,0:T(8,128)S(1)}, bf16[256,2048]{1,0:T(8,128)(2,1)S(1)}) custom-call(s32[1]{0:T(128)} %bitcast.me_ref, f32[3,2048]{1,0:T(4,128)S(1)} %copy-done.3, bf16[72,2048]{1,0:T(8,128)(2,1)S(1)} %get-tuple-element.45.refs_0_, bf16[72,2048]{1,0:T(8,128)(2,1)S(1)} %collective-permute-done.6.refs_1_, ...), custom_call_target="tpu_custom_call" | custom-call | flops 2048000000 | bytes 2048000000 | tf_op jit(solution)/shard_map/gram/pallas_call | solution.py:214
  39.2 3.1 %collective-permute-done.3.refs_1_ = bf16[72,1536]{1,0:T(8,128)(2,1)S(1)} collective-permute-done((bf16[72,1536]{1,0:T(8,128)(2,1)S(1)}, bf16[72,1536]{1,0:T(8,128)(2,1)S(1)}, u32[]{:S(2)}, u32[]{:S(2)}) %collective-permute-start.3) | collective-permute-done | bytes 221216 | tf_op jit(solution)/shard_map/ppermute | solution.py:423
  42.3 0.0 collective-permute-start.2
  42.3 3.1 %collective-permute-done.4.refs_2_ = bf16[72,1536]{1,0:T(8,128)(2,1)S(1)} collective-permute-done((bf16[72,1536]{1,0:T(8,128)(2,1)S(1)}, bf16[72,1536]{1,0:T(8,128)(2,1)S(1)}, u32[]{:S(2)}, u32[]{:S(2)}) %collective-permute-start.4) | collective-permute-done | bytes 221216 | tf_op jit(solution)/shard_map/ppermute | solution.py:423
  45.4 0.0 collective-permute-done.5.refs_3_
  45.4 1.0 %gram.6 = (f32[64,128]{1,0:T(8,128)S(1)}, bf16[256,1536]{1,0:T(8,128)(2,1)S(1)}) custom-call(s32[1]{0:T(128)} %bitcast.me_ref, f32[3,2048]{1,0:T(4,128)S(1)} %copy-done.3, bf16[72,1536]{1,0:T(8,128)(2,1)S(1)} %get-tuple-element.41.refs_0_, bf16[72,1536]{1,0:T(8,128)(2,1)S(1)} %collective-permute-done.3.refs_1_, ...), custom_call_target="tpu_custom_call" | custom-call | flops 1536000000 | bytes 1536000000 | tf_op jit(solution)/shard_map/gram/pallas_call | solution.py:214
  46.4 2.1 %collective-permute-done.refs_1_ = bf16[72,512]{1,0:T(8,128)(2,1)S(1)} collective-permute-done((bf16[72,512]{1,0:T(8,128)(2,1)S(1)}, bf16[72,512]{1,0:T(8,128)(2,1)S(1)}, u32[]{:S(2)}, u32[]{:S(2)}) %collective-permute-start) | collective-permute-done | bytes 73760 | tf_op jit(solution)/shard_map/ppermute | solution.py:423
  48.5 0.0 collective-permute-done.1.refs_2_
  48.5 0.0 collective-permute-done.2.refs_3_
  48.5 0.5 gram.7
  49.0 2.0 %collective-permute-start.12 = (f32[64,128]{1,0:T(8,128)S(1)}, f32[64,128]{1,0:T(8,128)S(1)}, u32[]{:S(2)}, u32[]{:S(2)}) collective-permute-start(f32[64,128]{1,0:T(8,128)S(1)} %get-tuple-element.56), channel_id=1, source_target_pairs={{0,1},{1,0},{2,3},{3,2},{4,5},{5,4},{6,7},{7,6},{8,9},{9,8},{10,11... | collective-permute-start | bytes 98312 | tf_op jit(solution)/shard_map/ppermute | solution.py:400
  51.0 0.9 %collective-permute-done.12 = f32[64,128]{1,0:T(8,128)S(1)} collective-permute-done((f32[64,128]{1,0:T(8,128)S(1)}, f32[64,128]{1,0:T(8,128)S(1)}, u32[]{:S(2)}, u32[]{:S(2)}) %collective-permute-start.12) | collective-permute-done | bytes 32800 | tf_op jit(solution)/shard_map/ppermute | solution.py:400
  51.9 1.9 %collective-permute-start.13 = (f32[64,128]{1,0:T(8,128)S(1)}, f32[64,128]{1,0:T(8,128)S(1)}, u32[]{:S(2)}, u32[]{:S(2)}) collective-permute-start(f32[64,128]{1,0:T(8,128)S(1)} %add.15), channel_id=1, source_target_pairs={{0,3},{1,2},{2,1},{3,0},{4,7},{5,6},{6,5},{7,4},{8,11},{9,10},{10,... | collective-permute-start | bytes 98312 | tf_op jit(solution)/shard_map/ppermute | solution.py:400
  53.7 1.6 %collective-permute-done.13 = f32[64,128]{1,0:T(8,128)S(1)} collective-permute-done((f32[64,128]{1,0:T(8,128)S(1)}, f32[64,128]{1,0:T(8,128)S(1)}, u32[]{:S(2)}, u32[]{:S(2)}) %collective-permute-start.13) | collective-permute-done | bytes 32800 | tf_op jit(solution)/shard_map/ppermute | solution.py:400
  55.3 3.9 %collective-permute-start.14 = (f32[64,128]{1,0:T(8,128)S(1)}, f32[64,128]{1,0:T(8,128)S(1)}, u32[]{:S(2)}, u32[]{:S(2)}) collective-permute-start(f32[64,128]{1,0:T(8,128)S(1)} %add.16), channel_id=1, source_target_pairs={{0,7},{1,6},{2,5},{3,4},{4,3},{5,2},{6,1},{7,0},{8,15},{9,14},{10,... | collective-permute-start | bytes 98312 | tf_op jit(solution)/shard_map/ppermute | solution.py:400
  59.2 1.6 %collective-permute-done.14 = f32[64,128]{1,0:T(8,128)S(1)} collective-permute-done((f32[64,128]{1,0:T(8,128)S(1)}, f32[64,128]{1,0:T(8,128)S(1)}, u32[]{:S(2)}, u32[]{:S(2)}) %collective-permute-start.14) | collective-permute-done | bytes 32800 | tf_op jit(solution)/shard_map/ppermute | solution.py:400
  60.8 1.4 %collective-permute-start.15 = (f32[64,128]{1,0:T(8,128)S(1)}, f32[64,128]{1,0:T(8,128)S(1)}, u32[]{:S(2)}, u32[]{:S(2)}) collective-permute-start(f32[64,128]{1,0:T(8,128)S(1)} %add.17), channel_id=1, source_target_pairs={{0,9},{1,8},{2,11},{3,10},{4,13},{5,12},{6,15},{7,14},{8,1},{9,0},... | collective-permute-start | bytes 98312 | tf_op jit(solution)/shard_map/ppermute | solution.py:400
  62.2 2.0 %collective-permute-done.15 = f32[64,128]{1,0:T(8,128)S(1)} collective-permute-done((f32[64,128]{1,0:T(8,128)S(1)}, f32[64,128]{1,0:T(8,128)S(1)}, u32[]{:S(2)}, u32[]{:S(2)}) %collective-permute-start.15) | collective-permute-done | bytes 32800 | tf_op jit(solution)/shard_map/ppermute | solution.py:400
  64.1 2.8 %collective-permute-start.16 = (f32[64,128]{1,0:T(8,128)S(1)}, f32[64,128]{1,0:T(8,128)S(1)}, u32[]{:S(2)}, u32[]{:S(2)}) collective-permute-start(f32[64,128]{1,0:T(8,128)S(1)} %add.18), channel_id=1, source_target_pairs={{0,25},{1,24},{2,27},{3,26},{4,29},{5,28},{6,31},{7,30},{8,17},{9,... | collective-permute-start | bytes 98312 | tf_op jit(solution)/shard_map/ppermute | solution.py:400
  66.9 1.8 %collective-permute-done.16 = f32[64,128]{1,0:T(8,128)S(1)} collective-permute-done((f32[64,128]{1,0:T(8,128)S(1)}, f32[64,128]{1,0:T(8,128)S(1)}, u32[]{:S(2)}, u32[]{:S(2)}) %collective-permute-start.16) | collective-permute-done | bytes 32800 | tf_op jit(solution)/shard_map/ppermute | solution.py:400
  68.7 4.9 %recon.1 = bf16[4,2,3,32,2048]{4,3,2,1,0:T(8,128)(2,1)} custom-call(f32[64,128]{1,0:T(8,128)S(1)} %add.19.total_ref, bf16[256,2048]{1,0:T(8,128)(2,1)S(1)} %get-tuple-element.57.refs_0_, bf16[256,2048]{1,0:T(8,128)(2,1)S(1)} %get-tuple-element.58.refs_1_, bf16[256,1536]{1,0:T(8,128)(2,1)S(1)} %get-tuple-element.59.refs_2_, ...), custom_call_target="tpu_custom_call" | custom-call | tf_op jit(solution)/shard_map/recon/pallas_call | solution.py:367
  (5 shorter events, 0.0 us)
Async XLA Ops:
  0.0 1.4 %copy-start = (bf16[128,3,2048]{2,0,1:T(8,128)(2,1)S(1)}, bf16[128,3,2048]{2,0,1:T(8,128)(2,1)}, u32[]{:S(2)}) copy-start(bf16[128,3,2048]{2,0,1:T(8,128)(2,1)} %param.5) | copy-start | bytes 4718596
  1.4 0.7 copy-start.2
  2.1 9.5 %copy-start.1 = (bf16[128,3,2048]{2,0,1:T(8,128)(2,1)S(1)}, bf16[128,3,2048]{2,0,1:T(8,128)(2,1)}, u32[]{:S(2)}) copy-start(bf16[128,3,2048]{2,0,1:T(8,128)(2,1)} %param.5) | copy-start | bytes 4718596
  5.8 11.1 %collective-permute-start.9 = (bf16[72,2048]{1,0:T(8,128)(2,1)S(1)}, bf16[72,2048]{1,0:T(8,128)(2,1)S(1)}, u32[]{:S(2)}, u32[]{:S(2)}) collective-permute-start(bf16[72,2048]{1,0:T(8,128)(2,1)S(1)} %get-tuple-element.50), channel_id=1, source_target_pairs={{0,32},{32,64},{64,96},{96,0},{1,33},{33,65},{65,97},{97,1},{2,34}... | collective-permute-start | bytes 884744 | tf_op jit(solution)/shard_map/ppermute | solution.py:423
  7.9 17.8 %collective-permute-start.10 = (bf16[72,2048]{1,0:T(8,128)(2,1)S(1)}, bf16[72,2048]{1,0:T(8,128)(2,1)S(1)}, u32[]{:S(2)}, u32[]{:S(2)}) collective-permute-start(bf16[72,2048]{1,0:T(8,128)(2,1)S(1)} %get-tuple-element.51), channel_id=1, source_target_pairs={{0,64},{32,96},{64,0},{96,32},{1,65},{33,97},{65,1},{97,33},{2,66}... | collective-permute-start | bytes 884744 | tf_op jit(solution)/shard_map/ppermute | solution.py:423
  10.4 15.9 %collective-permute-start.11 = (bf16[72,2048]{1,0:T(8,128)(2,1)S(1)}, bf16[72,2048]{1,0:T(8,128)(2,1)S(1)}, u32[]{:S(2)}, u32[]{:S(2)}) collective-permute-start(bf16[72,2048]{1,0:T(8,128)(2,1)S(1)} %get-tuple-element.52), channel_id=1, source_target_pairs={{0,96},{32,0},{64,32},{96,64},{1,97},{33,1},{65,33},{97,65},{2,98}... | collective-permute-start | bytes 884744 | tf_op jit(solution)/shard_map/ppermute | solution.py:423
  15.7 15.8 %collective-permute-start.6 = (bf16[72,2048]{1,0:T(8,128)(2,1)S(1)}, bf16[72,2048]{1,0:T(8,128)(2,1)S(1)}, u32[]{:S(2)}, u32[]{:S(2)}) collective-permute-start(bf16[72,2048]{1,0:T(8,128)(2,1)S(1)} %get-tuple-element.46), channel_id=1, source_target_pairs={{0,32},{32,64},{64,96},{96,0},{1,33},{33,65},{65,97},{97,1},{2,34}... | collective-permute-start | bytes 884744 | tf_op jit(solution)/shard_map/ppermute | solution.py:423
  16.1 19.8 %collective-permute-start.7 = (bf16[72,2048]{1,0:T(8,128)(2,1)S(1)}, bf16[72,2048]{1,0:T(8,128)(2,1)S(1)}, u32[]{:S(2)}, u32[]{:S(2)}) collective-permute-start(bf16[72,2048]{1,0:T(8,128)(2,1)S(1)} %get-tuple-element.47), channel_id=1, source_target_pairs={{0,64},{32,96},{64,0},{96,32},{1,65},{33,97},{65,1},{97,33},{2,66}... | collective-permute-start | bytes 884744 | tf_op jit(solution)/shard_map/ppermute | solution.py:423
  16.9 19.2 %collective-permute-start.8 = (bf16[72,2048]{1,0:T(8,128)(2,1)S(1)}, bf16[72,2048]{1,0:T(8,128)(2,1)S(1)}, u32[]{:S(2)}, u32[]{:S(2)}) collective-permute-start(bf16[72,2048]{1,0:T(8,128)(2,1)S(1)} %get-tuple-element.48), channel_id=1, source_target_pairs={{0,96},{32,0},{64,32},{96,64},{1,97},{33,1},{65,33},{97,65},{2,98}... | collective-permute-start | bytes 884744 | tf_op jit(solution)/shard_map/ppermute | solution.py:423
  22.7 8.8 %copy-start.3 = (f32[3,2048]{1,0:T(4,128)S(1)}, f32[3,2048]{1,0:T(4,128)}, u32[]{:S(2)}) copy-start(f32[3,2048]{1,0:T(4,128)} %weight_ref.7) | copy-start | bytes 73732
  25.8 16.5 %collective-permute-start.3 = (bf16[72,1536]{1,0:T(8,128)(2,1)S(1)}, bf16[72,1536]{1,0:T(8,128)(2,1)S(1)}, u32[]{:S(2)}, u32[]{:S(2)}) collective-permute-start(bf16[72,1536]{1,0:T(8,128)(2,1)S(1)} %get-tuple-element.42), channel_id=1, source_target_pairs={{0,32},{32,64},{64,96},{96,0},{1,33},{33,65},{65,97},{97,1},{2,34}... | collective-permute-start | bytes 663560 | tf_op jit(solution)/shard_map/ppermute | solution.py:423
  26.3 19.0 %collective-permute-start.4 = (bf16[72,1536]{1,0:T(8,128)(2,1)S(1)}, bf16[72,1536]{1,0:T(8,128)(2,1)S(1)}, u32[]{:S(2)}, u32[]{:S(2)}) collective-permute-start(bf16[72,1536]{1,0:T(8,128)(2,1)S(1)} %get-tuple-element.43), channel_id=1, source_target_pairs={{0,64},{32,96},{64,0},{96,32},{1,65},{33,97},{65,1},{97,33},{2,66}... | collective-permute-start | bytes 663560 | tf_op jit(solution)/shard_map/ppermute | solution.py:423
  31.5 13.9 %collective-permute-start.5 = (bf16[72,1536]{1,0:T(8,128)(2,1)S(1)}, bf16[72,1536]{1,0:T(8,128)(2,1)S(1)}, u32[]{:S(2)}, u32[]{:S(2)}) collective-permute-start(bf16[72,1536]{1,0:T(8,128)(2,1)S(1)} %get-tuple-element.44), channel_id=1, source_target_pairs={{0,96},{32,0},{64,32},{96,64},{1,97},{33,1},{65,33},{97,65},{2,98}... | collective-permute-start | bytes 663560 | tf_op jit(solution)/shard_map/ppermute | solution.py:423
  35.8 12.7 %collective-permute-start = (bf16[72,512]{1,0:T(8,128)(2,1)S(1)}, bf16[72,512]{1,0:T(8,128)(2,1)S(1)}, u32[]{:S(2)}, u32[]{:S(2)}) collective-permute-start(bf16[72,512]{1,0:T(8,128)(2,1)S(1)} %get-tuple-element.38), channel_id=1, source_target_pairs={{0,32},{32,64},{64,96},{96,0},{1,33},{33,65},{65,97},{97,1},{2,34}... | collective-permute-start | bytes 221192 | tf_op jit(solution)/shard_map/ppermute | solution.py:423
  36.1 12.5 %collective-permute-start.1 = (bf16[72,512]{1,0:T(8,128)(2,1)S(1)}, bf16[72,512]{1,0:T(8,128)(2,1)S(1)}, u32[]{:S(2)}, u32[]{:S(2)}) collective-permute-start(bf16[72,512]{1,0:T(8,128)(2,1)S(1)} %get-tuple-element.39), channel_id=1, source_target_pairs={{0,64},{32,96},{64,0},{96,32},{1,65},{33,97},{65,1},{97,33},{2,66}... | collective-permute-start | bytes 221192 | tf_op jit(solution)/shard_map/ppermute | solution.py:423
  42.3 6.3 %collective-permute-start.2 = (bf16[72,512]{1,0:T(8,128)(2,1)S(1)}, bf16[72,512]{1,0:T(8,128)(2,1)S(1)}, u32[]{:S(2)}, u32[]{:S(2)}) collective-permute-start(bf16[72,512]{1,0:T(8,128)(2,1)S(1)} %get-tuple-element.40), channel_id=1, source_target_pairs={{0,96},{32,0},{64,32},{96,64},{1,97},{33,1},{65,33},{97,65},{2,98}... | collective-permute-start | bytes 221192 | tf_op jit(solution)/shard_map/ppermute | solution.py:423
  49.0 2.8 %collective-permute-start.12 = (f32[64,128]{1,0:T(8,128)S(1)}, f32[64,128]{1,0:T(8,128)S(1)}, u32[]{:S(2)}, u32[]{:S(2)}) collective-permute-start(f32[64,128]{1,0:T(8,128)S(1)} %get-tuple-element.56), channel_id=1, source_target_pairs={{0,1},{1,0},{2,3},{3,2},{4,5},{5,4},{6,7},{7,6},{8,9},{9,8},{10,11... | collective-permute-start | bytes 98312 | tf_op jit(solution)/shard_map/ppermute | solution.py:400
  51.9 3.5 %collective-permute-start.13 = (f32[64,128]{1,0:T(8,128)S(1)}, f32[64,128]{1,0:T(8,128)S(1)}, u32[]{:S(2)}, u32[]{:S(2)}) collective-permute-start(f32[64,128]{1,0:T(8,128)S(1)} %add.15), channel_id=1, source_target_pairs={{0,3},{1,2},{2,1},{3,0},{4,7},{5,6},{6,5},{7,4},{8,11},{9,10},{10,... | collective-permute-start | bytes 98312 | tf_op jit(solution)/shard_map/ppermute | solution.py:400
  55.3 5.5 %collective-permute-start.14 = (f32[64,128]{1,0:T(8,128)S(1)}, f32[64,128]{1,0:T(8,128)S(1)}, u32[]{:S(2)}, u32[]{:S(2)}) collective-permute-start(f32[64,128]{1,0:T(8,128)S(1)} %add.16), channel_id=1, source_target_pairs={{0,7},{1,6},{2,5},{3,4},{4,3},{5,2},{6,1},{7,0},{8,15},{9,14},{10,... | collective-permute-start | bytes 98312 | tf_op jit(solution)/shard_map/ppermute | solution.py:400
  60.8 3.3 %collective-permute-start.15 = (f32[64,128]{1,0:T(8,128)S(1)}, f32[64,128]{1,0:T(8,128)S(1)}, u32[]{:S(2)}, u32[]{:S(2)}) collective-permute-start(f32[64,128]{1,0:T(8,128)S(1)} %add.17), channel_id=1, source_target_pairs={{0,9},{1,8},{2,11},{3,10},{4,13},{5,12},{6,15},{7,14},{8,1},{9,0},... | collective-permute-start | bytes 98312 | tf_op jit(solution)/shard_map/ppermute | solution.py:400
  64.1 4.6 %collective-permute-start.16 = (f32[64,128]{1,0:T(8,128)S(1)}, f32[64,128]{1,0:T(8,128)S(1)}, u32[]{:S(2)}, u32[]{:S(2)}) collective-permute-start(f32[64,128]{1,0:T(8,128)S(1)} %add.18), channel_id=1, source_target_pairs={{0,25},{1,24},{2,27},{3,26},{4,29},{5,28},{6,31},{7,30},{8,17},{9,... | collective-permute-start | bytes 98312 | tf_op jit(solution)/shard_map/ppermute | solution.py:400

commit v3 on v2

--- a/solution.py
+++ b/solution.py
@@ -11,7 +11,7 @@
 MODES = 4
 EIG_ITERS = 3
 TILE = 512
-CHUNKS = (2048, 2048, 1536, 512)
+CHUNKS = (1792, 1792, 1792, 768)
 COST = 1000000
 
 
@@ -124,7 +124,7 @@
     parts = pieces(start, width, points, TILE)
     vmem = pl.BlockSpec(memory_space=pltpu.VMEM)
     smem = pl.BlockSpec(memory_space=pltpu.SMEM)
-    hbm = pl.BlockSpec(memory_space=pl.ANY)
+    hbm = pl.BlockSpec(memory_space=pltpu.HBM)
     out_shape = [jax.ShapeDtypeStruct((72, width), jnp.bfloat16)] * 4
     scratch = [
         pltpu.VMEM((rows, width), jnp.bfloat16),
@@ -252,18 +252,27 @@
 
     def orthonormal(base):
         other = turn(base)
+        along, across = [], []
+        for k in range(MODES):
+            for vectors, result in ((base, along), (other, across)):
+                inner = jnp.sum(base * pick(vectors, k), axis=2, keepdims=True)
+                result.append(jnp.broadcast_to(inner, shape))
         for j in range(MODES):
+            scale = lax.rsqrt(pick(along[j], j))
+            square = scale * scale
+            a, b = along[j] * square, across[j] * square
+            for k in range(j + 1, MODES):
+                a_k, b_k = pick(a, k), pick(b, k)
+                along[k], across[k] = (
+                    along[k] - a_k * along[j] - b_k * across[j],
+                    across[k] - a_k * across[j] + b_k * along[j],
+                )
             one, two = pick(base, j), pick(other, j)
-            along = jnp.sum(base * one, axis=2, keepdims=True)
-            across = jnp.sum(base * two, axis=2, keepdims=True)
-            scale = lax.rsqrt(pick(along, j))
-            a, b = along * scale * scale, across * scale * scale
-            later = place > j
-            new_base = jnp.where(later, base - a * one - b * two, base)
-            new_other = jnp.where(later, other - a * two + b * one, other)
-            here = place == j
-            base = jnp.where(here, base * scale, new_base)
-            other = jnp.where(here, other * scale, new_other)
+            later, here = place > j, place == j
+            base, other = (
+                jnp.where(later, base - a * one - b * two, jnp.where(here, base * scale, base)),
+                jnp.where(later, other - a * two + b * one, jnp.where(here, other * scale, other)),
+            )
         return base, other
 
     def wide(left, right):
@@ -333,25 +342,28 @@
     sides, (out_ref, proj_ref, held, sems) = refs[:-4], refs[-4:]
     projections(total_ref, proj_ref)
     sends = []
-    for k, (side, at, comp, column, size) in enumerate(runs):
+    for comp in range(out_ref.shape[2]):
         for pair in range(2):
-            result = jnp.dot(
-                proj_ref[pair],
-                sides[side][128 * pair : 128 * pair + 128, at : at + size],
-                preferred_element_type=jnp.float32,
-            ).astype(jnp.bfloat16)
-            for freq in range(2):
-                for part in range(2):
-                    start = 64 * freq + 32 * part
-                    held[2 * pair + freq, part, comp, :, column : column + size] = result[
-                        start : start + 32
-                    ]
-        columns = pl.ds(column, size)
-        send = pltpu.make_async_copy(
-            held.at[:, :, comp, :, columns], out_ref.at[:, :, comp, :, columns], sems.at[k]
-        )
-        send.start()
-        sends.append(send)
+            freqs = slice(2 * pair, 2 * pair + 2)
+            for side, at, own_comp, column, size in runs:
+                if own_comp != comp:
+                    continue
+                result = jnp.dot(
+                    proj_ref[pair],
+                    sides[side][128 * pair : 128 * pair + 128, at : at + size],
+                    preferred_element_type=jnp.float32,
+                ).astype(jnp.bfloat16)
+                for freq in range(2):
+                    for part in range(2):
+                        start = 64 * freq + 32 * part
+                        held[2 * pair + freq, part, comp, :, column : column + size] = result[
+                            start : start + 32
+                        ]
+            send = pltpu.make_async_copy(
+                held.at[freqs, :, comp], out_ref.at[freqs, :, comp], sems.at[comp, pair]
+            )
+            send.start()
+            sends.append(send)
     for send in sends:
         send.wait()
 
@@ -372,7 +384,7 @@
         scratch_shapes=[
             pltpu.VMEM((2, 128, 128), jnp.bfloat16),
             pltpu.VMEM(shape, jnp.bfloat16),
-            pltpu.SemaphoreType.DMA((len(runs),)),
+            pltpu.SemaphoreType.DMA((comps, 2)),
         ],
         compiler_params=pltpu.CompilerParams(vmem_limit_bytes=32 * 2**20),
         name="recon",
@@ -405,6 +417,10 @@
     _, comps, points = snapshots.shape
     snapshots = jnp.transpose(snapshots, (1, 0, 2))
     tail = jnp.transpose(tail_rows, (1, 0, 2))
+    snapshots, tail, freq_bins = (
+        pltpu.with_memory_space_constraint(array, pltpu.HBM)
+        for array in (snapshots, tail, freq_bins)
+    )
     me = lax.axis_index("blk").astype(jnp.int32).reshape(1)
     band = edge = None
     token = me

time: 74 us -> 69.8 us (0.943)
  local copies, waits for them, and re-layouts: 2.07 us -> 0.01 us
  waiting for transfers between devices: 22.7 us -> 20.9 us
  Pallas kernels: 24 us -> 22.5 us
  starting transfers between devices: 24.6 us -> 25.9 us
    unnamed x8 -> x2, local copies, waits for them, and re-layouts: 2.07 us -> 0.01 us
    ppermute x12, waiting for transfers between devices: 14.9 us -> 13.1 us  [on_device(): parts.append(lax.ppermute(sent[shift], 'blk', pairs))]
    ppermute x12, starting transfers between devices: 12.8 us -> 14.4 us  [on_device(): parts.append(lax.ppermute(sent[shift], 'blk', pairs))]
    pallas_call x1, Pallas kernels: 4.89 us -> 3.34 us  [recon(): pl.pallas_call(functools.partial(recon_kernel, runs=runs), in_specs=[pl.B...]
  transfers between devices with their start and end apart: 17 -> 17, of which waited for: 11 -> 12; matrix products, arithmetic and copies ran while one was open for 0% -> 0% of each run, Pallas kernels for 20% -> 22%
where the time goes in v3:
time: 69.8 us; the launch traced here: 69.6 us
  starting transfers between devices  25.9 us (37%)
  Pallas kernels  22.5 us (32%)
  waiting for transfers between devices  20.9 us (30%)
    pallas_call x4, Pallas kernels, fourier(): pl.pallas_call(functools.partial(kernel, parts=parts), in_specs=in_specs...  15.4 us
    ppermute x12, starting transfers between devices, on_device(): parts.append(lax.ppermute(sent[shift], 'blk', pairs))  14.4 us
    ppermute x12, waiting for transfers between devices, on_device(): parts.append(lax.ppermute(sent[shift], 'blk', pairs))  13.1 us
    ppermute x5, starting transfers between devices, point_sum(): value = value + lax.ppermute(value, 'pts', pairs)  11.5 us
    ppermute x5, waiting for transfers between devices, point_sum(): value = value + lax.ppermute(value, 'pts', pairs)  7.8 us
    pallas_call x4, Pallas kernels, gram(): pl.pallas_call(functools.partial(gram_kernel, runs=pieces(start, width, w...  3.85 us
    pallas_call x1, Pallas kernels, recon(): pl.pallas_call(functools.partial(recon_kernel, runs=runs), in_specs=[pl.B...  3.34 us
  transfers between devices with their start and end apart: 17, of which 12 were waited for; matrix products, arithmetic and copies ran while one was open for 0% of the time, Pallas kernels for 22%

profile of v3, /device:TPU:1, one launch (start us, length us, event | category | flops | bytes accessed | tf_op | source)
XLA Modules:
  0.0 69.6 jit_solution(10171042153386249303)
XLA Ops:
  0.0 3.5 %fourier.4 = (bf16[72,1792]{1,0:T(8,128)(2,1)S(1)}, bf16[72,1792]{1,0:T(8,128)(2,1)S(1)}, bf16[72,1792]{1,0:T(8,128)(2,1)S(1)}, bf16[72,1792]{1,0:T(8,128)(2,1)S...) custom-call(s32[1]{0:T(128)} %bitcast.me_ref, s32[16]{0:T(128)} %freq_ref.1, ...), custom_call_target="tpu_custom_call" | custom-call | flops 1792000000 | bytes 1792000000 | tf_op jit(solution)/shard_map/fourier/pallas_call | solution.py:151
  3.5 2.1 %collective-permute-start.9 = (bf16[72,1792]{1,0:T(8,128)(2,1)S(1)}, bf16[72,1792]{1,0:T(8,128)(2,1)S(1)}, u32[]{:S(2)}, u32[]{:S(2)}) collective-permute-start(bf16[72,1792]{1,0:T(8,128)(2,1)S(1)} %get-tuple-element.50), channel_id=1, source_target_pairs={{0,32},{32,64},{64,96},{96,0},{1,33},{33,65},{65,97},{97,1},{2,34}... | collective-permute-start | bytes 774152 | tf_op jit(solution)/shard_map/ppermute | solution.py:439
  5.6 2.5 %collective-permute-start.10 = (bf16[72,1792]{1,0:T(8,128)(2,1)S(1)}, bf16[72,1792]{1,0:T(8,128)(2,1)S(1)}, u32[]{:S(2)}, u32[]{:S(2)}) collective-permute-start(bf16[72,1792]{1,0:T(8,128)(2,1)S(1)} %get-tuple-element.51), channel_id=1, source_target_pairs={{0,64},{32,96},{64,0},{96,32},{1,65},{33,97},{65,1},{97,33},{2,66}... | collective-permute-start | bytes 774152 | tf_op jit(solution)/shard_map/ppermute | solution.py:439
  8.0 1.2 %collective-permute-start.11 = (bf16[72,1792]{1,0:T(8,128)(2,1)S(1)}, bf16[72,1792]{1,0:T(8,128)(2,1)S(1)}, u32[]{:S(2)}, u32[]{:S(2)}) collective-permute-start(bf16[72,1792]{1,0:T(8,128)(2,1)S(1)} %get-tuple-element.52), channel_id=1, source_target_pairs={{0,96},{32,0},{64,32},{96,64},{1,97},{33,1},{65,33},{97,65},{2,98}... | collective-permute-start | bytes 774152 | tf_op jit(solution)/shard_map/ppermute | solution.py:439
  9.2 3.8 %fourier.5 = (bf16[72,1792]{1,0:T(8,128)(2,1)S(1)}, bf16[72,1792]{1,0:T(8,128)(2,1)S(1)}, bf16[72,1792]{1,0:T(8,128)(2,1)S(1)}, bf16[72,1792]{1,0:T(8,128)(2,1)S(1)}, s32[1]{0:T(128)}) custom-call(s32[1]{0:T(128)} %bitcast.me_ref, bf16[256,1024]{1,0:T(8,128)(2,1)S(1)} %get-tuple-element.33.band_ref, bf16[32,128]{1,0:T(8,128)(2,1)S(1)} %get-tuple-element.34.edge_ref, ...), custom_call_target="tpu_custom_call" | custom-call | flops 1792000000 | bytes 1792000000 | tf_op jit(solution)/shard_map/fourier/pallas_call | solution.py:151
  13.0 0.4 collective-permute-start.6
  13.4 0.9 %collective-permute-start.7 = (bf16[72,1792]{1,0:T(8,128)(2,1)S(1)}, bf16[72,1792]{1,0:T(8,128)(2,1)S(1)}, u32[]{:S(2)}, u32[]{:S(2)}) collective-permute-start(bf16[72,1792]{1,0:T(8,128)(2,1)S(1)} %get-tuple-element.47), channel_id=1, source_target_pairs={{0,64},{32,96},{64,0},{96,32},{1,65},{33,97},{65,1},{97,33},{2,66}... | collective-permute-start | bytes 774152 | tf_op jit(solution)/shard_map/ppermute | solution.py:439
  14.3 0.0 collective-permute-done.9.refs_1_
  14.3 1.6 %collective-permute-start.8 = (bf16[72,1792]{1,0:T(8,128)(2,1)S(1)}, bf16[72,1792]{1,0:T(8,128)(2,1)S(1)}, u32[]{:S(2)}, u32[]{:S(2)}) collective-permute-start(bf16[72,1792]{1,0:T(8,128)(2,1)S(1)} %get-tuple-element.48), channel_id=1, source_target_pairs={{0,96},{32,0},{64,32},{96,64},{1,97},{33,1},{65,33},{97,65},{2,98}... | collective-permute-start | bytes 774152 | tf_op jit(solution)/shard_map/ppermute | solution.py:439
  15.9 4.6 %fourier.6 = (bf16[72,1792]{1,0:T(8,128)(2,1)S(1)}, bf16[72,1792]{1,0:T(8,128)(2,1)S(1)}, bf16[72,1792]{1,0:T(8,128)(2,1)S(1)}, bf16[72,1792]{1,0:T(8,128)(2,1)S(1)}, s32[1]{0:T(128)}) custom-call(s32[1]{0:T(128)} %get-tuple-element.35.me_ref, bf16[256,1024]{1,0:T(8,128)(2,1)S(1)} %get-tuple-element.33.band_ref, ...), custom_call_target="tpu_custom_call" | custom-call | flops 1792000000 | bytes 1792000000 | tf_op jit(solution)/shard_map/fourier/pallas_call | solution.py:151
  20.5 0.0 copy-start
  20.5 3.5 %fourier.7 = (bf16[72,768]{1,0:T(8,128)(2,1)S(1)}, bf16[72,768]{1,0:T(8,128)(2,1)S(1)}, bf16[72,768]{1,0:T(8,128)(2,1)S(1)}, bf16[72,768]{1,0:T(8,128)(2,1)S(1)}, s32[1]{0:T(128)}) custom-call(s32[1]{0:T(128)} %get-tuple-element.36.me_ref, bf16[256,1024]{1,0:T(8,128)(2,1)S(1)} %get-tuple-element.33.band_ref, bf16[32,128]{1,0:T(8,128)(2,1)S(1)} %get-tuple-element.34.edge_ref, ...), custom_call_target="tpu_custom_call" | custom-call | flops 768000000 | bytes 768000000 | tf_op jit(solution)/shard_map/fourier/pallas_call | solution.py:151
  24.0 0.0 collective-permute-done.10.refs_2_
  24.0 0.5 collective-permute-start.3
  24.5 0.0 collective-permute-done.11.refs_3_
  24.5 1.9 %collective-permute-start.4 = (bf16[72,1792]{1,0:T(8,128)(2,1)S(1)}, bf16[72,1792]{1,0:T(8,128)(2,1)S(1)}, u32[]{:S(2)}, u32[]{:S(2)}) collective-permute-start(bf16[72,1792]{1,0:T(8,128)(2,1)S(1)} %get-tuple-element.43), channel_id=1, source_target_pairs={{0,64},{32,96},{64,0},{96,32},{1,65},{33,97},{65,1},{97,33},{2,66}... | collective-permute-start | bytes 774152 | tf_op jit(solution)/shard_map/ppermute | solution.py:439
  26.4 0.4 collective-permute-done.6.refs_1_
  26.8 1.6 %collective-permute-start.5 = (bf16[72,1792]{1,0:T(8,128)(2,1)S(1)}, bf16[72,1792]{1,0:T(8,128)(2,1)S(1)}, u32[]{:S(2)}, u32[]{:S(2)}) collective-permute-start(bf16[72,1792]{1,0:T(8,128)(2,1)S(1)} %get-tuple-element.44), channel_id=1, source_target_pairs={{0,96},{32,0},{64,32},{96,64},{1,97},{33,1},{65,33},{97,65},{2,98}... | collective-permute-start | bytes 774152 | tf_op jit(solution)/shard_map/ppermute | solution.py:439
  28.4 0.0 copy-done
  28.4 1.1 %gram.4 = (f32[64,128]{1,0:T(8,128)S(1)}, bf16[256,1792]{1,0:T(8,128)(2,1)S(1)}) custom-call(s32[1]{0:T(128)} %bitcast.me_ref, f32[3,2048]{1,0:T(4,128)S(1)} %copy-done, bf16[72,1792]{1,0:T(8,128)(2,1)S(1)} %get-tuple-element.49.refs_0_, bf16[72,1792]{1,0:T(8,128)(2,1)S(1)} %collective-permute-done.9.refs_1_, ...), custom_call_target="tpu_custom_call" | custom-call | flops 1792000000 | bytes 1792000000 | tf_op jit(solution)/shard_map/gram/pallas_call | solution.py:214
  29.5 0.9 %collective-permute-done.7.refs_2_ = bf16[72,1792]{1,0:T(8,128)(2,1)S(1)} collective-permute-done((bf16[72,1792]{1,0:T(8,128)(2,1)S(1)}, bf16[72,1792]{1,0:T(8,128)(2,1)S(1)}, u32[]{:S(2)}, u32[]{:S(2)}) %collective-permute-start.7) | collective-permute-done | bytes 258080 | tf_op jit(solution)/shard_map/ppermute | solution.py:439
  30.3 0.0 collective-permute-start
  30.3 0.3 collective-permute-done.8.refs_3_
  30.6 1.8 %collective-permute-start.1 = (bf16[72,768]{1,0:T(8,128)(2,1)S(1)}, bf16[72,768]{1,0:T(8,128)(2,1)S(1)}, u32[]{:S(2)}, u32[]{:S(2)}) collective-permute-start(bf16[72,768]{1,0:T(8,128)(2,1)S(1)} %get-tuple-element.39), channel_id=1, source_target_pairs={{0,64},{32,96},{64,0},{96,32},{1,65},{33,97},{65,1},{97,33},{2,66}... | collective-permute-start | bytes 331784 | tf_op jit(solution)/shard_map/ppermute | solution.py:439
  32.4 1.1 %gram.5 = (f32[64,128]{1,0:T(8,128)S(1)}, bf16[256,1792]{1,0:T(8,128)(2,1)S(1)}) custom-call(s32[1]{0:T(128)} %bitcast.me_ref, f32[3,2048]{1,0:T(4,128)S(1)} %copy-done, bf16[72,1792]{1,0:T(8,128)(2,1)S(1)} %get-tuple-element.45.refs_0_, bf16[72,1792]{1,0:T(8,128)(2,1)S(1)} %collective-permute-done.6.refs_1_, ...), custom_call_target="tpu_custom_call" | custom-call | flops 1792000000 | bytes 1792000000 | tf_op jit(solution)/shard_map/gram/pallas_call | solution.py:214
  33.5 4.3 %collective-permute-done.3.refs_1_ = bf16[72,1792]{1,0:T(8,128)(2,1)S(1)} collective-permute-done((bf16[72,1792]{1,0:T(8,128)(2,1)S(1)}, bf16[72,1792]{1,0:T(8,128)(2,1)S(1)}, u32[]{:S(2)}, u32[]{:S(2)}) %collective-permute-start.3) | collective-permute-done | bytes 258080 | tf_op jit(solution)/shard_map/ppermute | solution.py:439
  37.8 0.0 collective-permute-start.2
  37.8 3.6 %collective-permute-done.4.refs_2_ = bf16[72,1792]{1,0:T(8,128)(2,1)S(1)} collective-permute-done((bf16[72,1792]{1,0:T(8,128)(2,1)S(1)}, bf16[72,1792]{1,0:T(8,128)(2,1)S(1)}, u32[]{:S(2)}, u32[]{:S(2)}) %collective-permute-start.4) | collective-permute-done | bytes 258080 | tf_op jit(solution)/shard_map/ppermute | solution.py:439
  41.4 0.0 collective-permute-done.5.refs_3_
  41.5 1.1 %gram.6 = (f32[64,128]{1,0:T(8,128)S(1)}, bf16[256,1792]{1,0:T(8,128)(2,1)S(1)}) custom-call(s32[1]{0:T(128)} %bitcast.me_ref, f32[3,2048]{1,0:T(4,128)S(1)} %copy-done, bf16[72,1792]{1,0:T(8,128)(2,1)S(1)} %get-tuple-element.41.refs_0_, bf16[72,1792]{1,0:T(8,128)(2,1)S(1)} %collective-permute-done.3.refs_1_, ...), custom_call_target="tpu_custom_call" | custom-call | flops 1792000000 | bytes 1792000000 | tf_op jit(solution)/shard_map/gram/pallas_call | solution.py:214
  42.5 3.2 %collective-permute-done.refs_1_ = bf16[72,768]{1,0:T(8,128)(2,1)S(1)} collective-permute-done((bf16[72,768]{1,0:T(8,128)(2,1)S(1)}, bf16[72,768]{1,0:T(8,128)(2,1)S(1)}, u32[]{:S(2)}, u32[]{:S(2)}) %collective-permute-start) | collective-permute-done | bytes 110624 | tf_op jit(solution)/shard_map/ppermute | solution.py:439
  45.7 0.5 collective-permute-done.1.refs_2_
  46.2 0.0 collective-permute-done.2.refs_3_
  46.2 0.6 gram.7
  46.8 1.6 %collective-permute-start.12 = (f32[64,128]{1,0:T(8,128)S(1)}, f32[64,128]{1,0:T(8,128)S(1)}, u32[]{:S(2)}, u32[]{:S(2)}) collective-permute-start(f32[64,128]{1,0:T(8,128)S(1)} %get-tuple-element.56), channel_id=1, source_target_pairs={{0,1},{1,0},{2,3},{3,2},{4,5},{5,4},{6,7},{7,6},{8,9},{9,8},{10,11... | collective-permute-start | bytes 98312 | tf_op jit(solution)/shard_map/ppermute | solution.py:412
  48.4 0.9 %collective-permute-done.12 = f32[64,128]{1,0:T(8,128)S(1)} collective-permute-done((f32[64,128]{1,0:T(8,128)S(1)}, f32[64,128]{1,0:T(8,128)S(1)}, u32[]{:S(2)}, u32[]{:S(2)}) %collective-permute-start.12) | collective-permute-done | bytes 32800 | tf_op jit(solution)/shard_map/ppermute | solution.py:412
  49.3 1.9 %collective-permute-start.13 = (f32[64,128]{1,0:T(8,128)S(1)}, f32[64,128]{1,0:T(8,128)S(1)}, u32[]{:S(2)}, u32[]{:S(2)}) collective-permute-start(f32[64,128]{1,0:T(8,128)S(1)} %add.15), channel_id=1, source_target_pairs={{0,3},{1,2},{2,1},{3,0},{4,7},{5,6},{6,5},{7,4},{8,11},{9,10},{10,... | collective-permute-start | bytes 98312 | tf_op jit(solution)/shard_map/ppermute | solution.py:412
  51.1 1.6 %collective-permute-done.13 = f32[64,128]{1,0:T(8,128)S(1)} collective-permute-done((f32[64,128]{1,0:T(8,128)S(1)}, f32[64,128]{1,0:T(8,128)S(1)}, u32[]{:S(2)}, u32[]{:S(2)}) %collective-permute-start.13) | collective-permute-done | bytes 32800 | tf_op jit(solution)/shard_map/ppermute | solution.py:412
  52.8 3.9 %collective-permute-start.14 = (f32[64,128]{1,0:T(8,128)S(1)}, f32[64,128]{1,0:T(8,128)S(1)}, u32[]{:S(2)}, u32[]{:S(2)}) collective-permute-start(f32[64,128]{1,0:T(8,128)S(1)} %add.16), channel_id=1, source_target_pairs={{0,7},{1,6},{2,5},{3,4},{4,3},{5,2},{6,1},{7,0},{8,15},{9,14},{10,... | collective-permute-start | bytes 98312 | tf_op jit(solution)/shard_map/ppermute | solution.py:412
  56.6 1.6 %collective-permute-done.14 = f32[64,128]{1,0:T(8,128)S(1)} collective-permute-done((f32[64,128]{1,0:T(8,128)S(1)}, f32[64,128]{1,0:T(8,128)S(1)}, u32[]{:S(2)}, u32[]{:S(2)}) %collective-permute-start.14) | collective-permute-done | bytes 32800 | tf_op jit(solution)/shard_map/ppermute | solution.py:412
  58.2 1.4 %collective-permute-start.15 = (f32[64,128]{1,0:T(8,128)S(1)}, f32[64,128]{1,0:T(8,128)S(1)}, u32[]{:S(2)}, u32[]{:S(2)}) collective-permute-start(f32[64,128]{1,0:T(8,128)S(1)} %add.17), channel_id=1, source_target_pairs={{0,9},{1,8},{2,11},{3,10},{4,13},{5,12},{6,15},{7,14},{8,1},{9,0},... | collective-permute-start | bytes 98312 | tf_op jit(solution)/shard_map/ppermute | solution.py:412
  59.6 2.0 %collective-permute-done.15 = f32[64,128]{1,0:T(8,128)S(1)} collective-permute-done((f32[64,128]{1,0:T(8,128)S(1)}, f32[64,128]{1,0:T(8,128)S(1)}, u32[]{:S(2)}, u32[]{:S(2)}) %collective-permute-start.15) | collective-permute-done | bytes 32800 | tf_op jit(solution)/shard_map/ppermute | solution.py:412
  61.6 2.8 %collective-permute-start.16 = (f32[64,128]{1,0:T(8,128)S(1)}, f32[64,128]{1,0:T(8,128)S(1)}, u32[]{:S(2)}, u32[]{:S(2)}) collective-permute-start(f32[64,128]{1,0:T(8,128)S(1)} %add.18), channel_id=1, source_target_pairs={{0,25},{1,24},{2,27},{3,26},{4,29},{5,28},{6,31},{7,30},{8,17},{9,... | collective-permute-start | bytes 98312 | tf_op jit(solution)/shard_map/ppermute | solution.py:412
  64.4 1.8 %collective-permute-done.16 = f32[64,128]{1,0:T(8,128)S(1)} collective-permute-done((f32[64,128]{1,0:T(8,128)S(1)}, f32[64,128]{1,0:T(8,128)S(1)}, u32[]{:S(2)}, u32[]{:S(2)}) %collective-permute-start.16) | collective-permute-done | bytes 32800 | tf_op jit(solution)/shard_map/ppermute | solution.py:412
  66.1 3.3 %recon.1 = bf16[4,2,3,32,2048]{4,3,2,1,0:T(8,128)(2,1)} custom-call(f32[64,128]{1,0:T(8,128)S(1)} %add.19.total_ref, bf16[256,1792]{1,0:T(8,128)(2,1)S(1)} %get-tuple-element.57.refs_0_, bf16[256,1792]{1,0:T(8,128)(2,1)S(1)} %get-tuple-element.58.refs_1_, bf16[256,1792]{1,0:T(8,128)(2,1)S(1)} %get-tuple-element.59.refs_2_, ...), custom_call_target="tpu_custom_call" | custom-call | tf_op jit(solution)/shard_map/recon/pallas_call | solution.py:379
  (5 shorter events, 0.0 us)
Async XLA Ops:
  3.5 10.8 %collective-permute-start.9 = (bf16[72,1792]{1,0:T(8,128)(2,1)S(1)}, bf16[72,1792]{1,0:T(8,128)(2,1)S(1)}, u32[]{:S(2)}, u32[]{:S(2)}) collective-permute-start(bf16[72,1792]{1,0:T(8,128)(2,1)S(1)} %get-tuple-element.50), channel_id=1, source_target_pairs={{0,32},{32,64},{64,96},{96,0},{1,33},{33,65},{65,97},{97,1},{2,34}... | collective-permute-start | bytes 774152 | tf_op jit(solution)/shard_map/ppermute | solution.py:439
  5.6 18.4 %collective-permute-start.10 = (bf16[72,1792]{1,0:T(8,128)(2,1)S(1)}, bf16[72,1792]{1,0:T(8,128)(2,1)S(1)}, u32[]{:S(2)}, u32[]{:S(2)}) collective-permute-start(bf16[72,1792]{1,0:T(8,128)(2,1)S(1)} %get-tuple-element.51), channel_id=1, source_target_pairs={{0,64},{32,96},{64,0},{96,32},{1,65},{33,97},{65,1},{97,33},{2,66}... | collective-permute-start | bytes 774152 | tf_op jit(solution)/shard_map/ppermute | solution.py:439
  8.0 16.5 %collective-permute-start.11 = (bf16[72,1792]{1,0:T(8,128)(2,1)S(1)}, bf16[72,1792]{1,0:T(8,128)(2,1)S(1)}, u32[]{:S(2)}, u32[]{:S(2)}) collective-permute-start(bf16[72,1792]{1,0:T(8,128)(2,1)S(1)} %get-tuple-element.52), channel_id=1, source_target_pairs={{0,96},{32,0},{64,32},{96,64},{1,97},{33,1},{65,33},{97,65},{2,98}... | collective-permute-start | bytes 774152 | tf_op jit(solution)/shard_map/ppermute | solution.py:439
  13.0 13.8 %collective-permute-start.6 = (bf16[72,1792]{1,0:T(8,128)(2,1)S(1)}, bf16[72,1792]{1,0:T(8,128)(2,1)S(1)}, u32[]{:S(2)}, u32[]{:S(2)}) collective-permute-start(bf16[72,1792]{1,0:T(8,128)(2,1)S(1)} %get-tuple-element.46), channel_id=1, source_target_pairs={{0,32},{32,64},{64,96},{96,0},{1,33},{33,65},{65,97},{97,1},{2,34}... | collective-permute-start | bytes 774152 | tf_op jit(solution)/shard_map/ppermute | solution.py:439
  13.4 17.0 %collective-permute-start.7 = (bf16[72,1792]{1,0:T(8,128)(2,1)S(1)}, bf16[72,1792]{1,0:T(8,128)(2,1)S(1)}, u32[]{:S(2)}, u32[]{:S(2)}) collective-permute-start(bf16[72,1792]{1,0:T(8,128)(2,1)S(1)} %get-tuple-element.47), channel_id=1, source_target_pairs={{0,64},{32,96},{64,0},{96,32},{1,65},{33,97},{65,1},{97,33},{2,66}... | collective-permute-start | bytes 774152 | tf_op jit(solution)/shard_map/ppermute | solution.py:439
  14.3 16.3 %collective-permute-start.8 = (bf16[72,1792]{1,0:T(8,128)(2,1)S(1)}, bf16[72,1792]{1,0:T(8,128)(2,1)S(1)}, u32[]{:S(2)}, u32[]{:S(2)}) collective-permute-start(bf16[72,1792]{1,0:T(8,128)(2,1)S(1)} %get-tuple-element.48), channel_id=1, source_target_pairs={{0,96},{32,0},{64,32},{96,64},{1,97},{33,1},{65,33},{97,65},{2,98}... | collective-permute-start | bytes 774152 | tf_op jit(solution)/shard_map/ppermute | solution.py:439
  20.5 7.9 %copy-start = (f32[3,2048]{1,0:T(4,128)S(1)}, f32[3,2048]{1,0:T(4,128)}, u32[]{:S(2)}) copy-start(f32[3,2048]{1,0:T(4,128)} %weight_ref.7) | copy-start | bytes 73732
  24.0 13.9 %collective-permute-start.3 = (bf16[72,1792]{1,0:T(8,128)(2,1)S(1)}, bf16[72,1792]{1,0:T(8,128)(2,1)S(1)}, u32[]{:S(2)}, u32[]{:S(2)}) collective-permute-start(bf16[72,1792]{1,0:T(8,128)(2,1)S(1)} %get-tuple-element.42), channel_id=1, source_target_pairs={{0,32},{32,64},{64,96},{96,0},{1,33},{33,65},{65,97},{97,1},{2,34}... | collective-permute-start | bytes 774152 | tf_op jit(solution)/shard_map/ppermute | solution.py:439
  24.5 16.9 %collective-permute-start.4 = (bf16[72,1792]{1,0:T(8,128)(2,1)S(1)}, bf16[72,1792]{1,0:T(8,128)(2,1)S(1)}, u32[]{:S(2)}, u32[]{:S(2)}) collective-permute-start(bf16[72,1792]{1,0:T(8,128)(2,1)S(1)} %get-tuple-element.43), channel_id=1, source_target_pairs={{0,64},{32,96},{64,0},{96,32},{1,65},{33,97},{65,1},{97,33},{2,66}... | collective-permute-start | bytes 774152 | tf_op jit(solution)/shard_map/ppermute | solution.py:439
  26.8 14.7 %collective-permute-start.5 = (bf16[72,1792]{1,0:T(8,128)(2,1)S(1)}, bf16[72,1792]{1,0:T(8,128)(2,1)S(1)}, u32[]{:S(2)}, u32[]{:S(2)}) collective-permute-start(bf16[72,1792]{1,0:T(8,128)(2,1)S(1)} %get-tuple-element.44), channel_id=1, source_target_pairs={{0,96},{32,0},{64,32},{96,64},{1,97},{33,1},{65,33},{97,65},{2,98}... | collective-permute-start | bytes 774152 | tf_op jit(solution)/shard_map/ppermute | solution.py:439
  30.3 15.4 %collective-permute-start = (bf16[72,768]{1,0:T(8,128)(2,1)S(1)}, bf16[72,768]{1,0:T(8,128)(2,1)S(1)}, u32[]{:S(2)}, u32[]{:S(2)}) collective-permute-start(bf16[72,768]{1,0:T(8,128)(2,1)S(1)} %get-tuple-element.38), channel_id=1, source_target_pairs={{0,32},{32,64},{64,96},{96,0},{1,33},{33,65},{65,97},{97,1},{2,34}... | collective-permute-start | bytes 331784 | tf_op jit(solution)/shard_map/ppermute | solution.py:439
  30.6 15.6 %collective-permute-start.1 = (bf16[72,768]{1,0:T(8,128)(2,1)S(1)}, bf16[72,768]{1,0:T(8,128)(2,1)S(1)}, u32[]{:S(2)}, u32[]{:S(2)}) collective-permute-start(bf16[72,768]{1,0:T(8,128)(2,1)S(1)} %get-tuple-element.39), channel_id=1, source_target_pairs={{0,64},{32,96},{64,0},{96,32},{1,65},{33,97},{65,1},{97,33},{2,66}... | collective-permute-start | bytes 331784 | tf_op jit(solution)/shard_map/ppermute | solution.py:439
  37.8 8.3 %collective-permute-start.2 = (bf16[72,768]{1,0:T(8,128)(2,1)S(1)}, bf16[72,768]{1,0:T(8,128)(2,1)S(1)}, u32[]{:S(2)}, u32[]{:S(2)}) collective-permute-start(bf16[72,768]{1,0:T(8,128)(2,1)S(1)} %get-tuple-element.40), channel_id=1, source_target_pairs={{0,96},{32,0},{64,32},{96,64},{1,97},{33,1},{65,33},{97,65},{2,98}... | collective-permute-start | bytes 331784 | tf_op jit(solution)/shard_map/ppermute | solution.py:439
  46.8 2.5 %collective-permute-start.12 = (f32[64,128]{1,0:T(8,128)S(1)}, f32[64,128]{1,0:T(8,128)S(1)}, u32[]{:S(2)}, u32[]{:S(2)}) collective-permute-start(f32[64,128]{1,0:T(8,128)S(1)} %get-tuple-element.56), channel_id=1, source_target_pairs={{0,1},{1,0},{2,3},{3,2},{4,5},{5,4},{6,7},{7,6},{8,9},{9,8},{10,11... | collective-permute-start | bytes 98312 | tf_op jit(solution)/shard_map/ppermute | solution.py:412
  49.3 3.5 %collective-permute-start.13 = (f32[64,128]{1,0:T(8,128)S(1)}, f32[64,128]{1,0:T(8,128)S(1)}, u32[]{:S(2)}, u32[]{:S(2)}) collective-permute-start(f32[64,128]{1,0:T(8,128)S(1)} %add.15), channel_id=1, source_target_pairs={{0,3},{1,2},{2,1},{3,0},{4,7},{5,6},{6,5},{7,4},{8,11},{9,10},{10,... | collective-permute-start | bytes 98312 | tf_op jit(solution)/shard_map/ppermute | solution.py:412
  52.8 5.5 %collective-permute-start.14 = (f32[64,128]{1,0:T(8,128)S(1)}, f32[64,128]{1,0:T(8,128)S(1)}, u32[]{:S(2)}, u32[]{:S(2)}) collective-permute-start(f32[64,128]{1,0:T(8,128)S(1)} %add.16), channel_id=1, source_target_pairs={{0,7},{1,6},{2,5},{3,4},{4,3},{5,2},{6,1},{7,0},{8,15},{9,14},{10,... | collective-permute-start | bytes 98312 | tf_op jit(solution)/shard_map/ppermute | solution.py:412
  58.2 3.3 %collective-permute-start.15 = (f32[64,128]{1,0:T(8,128)S(1)}, f32[64,128]{1,0:T(8,128)S(1)}, u32[]{:S(2)}, u32[]{:S(2)}) collective-permute-start(f32[64,128]{1,0:T(8,128)S(1)} %add.17), channel_id=1, source_target_pairs={{0,9},{1,8},{2,11},{3,10},{4,13},{5,12},{6,15},{7,14},{8,1},{9,0},... | collective-permute-start | bytes 98312 | tf_op jit(solution)/shard_map/ppermute | solution.py:412
  61.6 4.6 %collective-permute-start.16 = (f32[64,128]{1,0:T(8,128)S(1)}, f32[64,128]{1,0:T(8,128)S(1)}, u32[]{:S(2)}, u32[]{:S(2)}) collective-permute-start(f32[64,128]{1,0:T(8,128)S(1)} %add.18), channel_id=1, source_target_pairs={{0,25},{1,24},{2,27},{3,26},{4,29},{5,28},{6,31},{7,30},{8,17},{9,... | collective-permute-start | bytes 98312 | tf_op jit(solution)/shard_map/ppermute | solution.py:412

commit v4 on v3

--- a/solution.py
+++ b/solution.py
@@ -122,6 +122,12 @@
     comps, rows, points = snapshots.shape
     half = tail.shape[1]
     parts = pieces(start, width, points, TILE)
+    if band is None and width % TILE:
+        first = width % TILE
+        parts = [(0, 0, 0, first)] + [
+            (at + first, comp, column + first, size)
+            for at, comp, column, size in pieces(start, width - first, points, TILE)
+        ]
     vmem = pl.BlockSpec(memory_space=pltpu.VMEM)
     smem = pl.BlockSpec(memory_space=pltpu.SMEM)
     hbm = pl.BlockSpec(memory_space=pltpu.HBM)

time: 69.8 us -> 69.7 us (level)
  no operation moved by 1% of the time
where the time goes in v4:
time: 69.7 us; the launch traced here: 69.5 us
  starting transfers between devices  25.9 us (37%)
  Pallas kernels  22.4 us (32%)
  waiting for transfers between devices  20.9 us (30%)
    pallas_call x4, Pallas kernels, fourier(): pl.pallas_call(functools.partial(kernel, parts=parts), in_specs=in_specs...  15.2 us
    ppermute x12, starting transfers between devices, on_device(): parts.append(lax.ppermute(sent[shift], 'blk', pairs))  14.4 us
    ppermute x12, waiting for transfers between devices, on_device(): parts.append(lax.ppermute(sent[shift], 'blk', pairs))  13.1 us
    ppermute x5, starting transfers between devices, point_sum(): value = value + lax.ppermute(value, 'pts', pairs)  11.5 us
    ppermute x5, waiting for transfers between devices, point_sum(): value = value + lax.ppermute(value, 'pts', pairs)  7.81 us
    pallas_call x4, Pallas kernels, gram(): pl.pallas_call(functools.partial(gram_kernel, runs=pieces(start, width, w...  3.85 us
    pallas_call x1, Pallas kernels, recon(): pl.pallas_call(functools.partial(recon_kernel, runs=runs), in_specs=[pl.B...  3.34 us
  transfers between devices with their start and end apart: 17, of which 12 were waited for; matrix products, arithmetic and copies ran while one was open for 0% of the time, Pallas kernels for 22%

profile of v4, /device:TPU:1, one launch (start us, length us, event | category | flops | bytes accessed | tf_op | source)
XLA Modules:
  0.0 69.5 jit_solution(11001159785650711942)
XLA Ops:
  0.0 3.3 %fourier.4 = (bf16[72,1792]{1,0:T(8,128)(2,1)S(1)}, bf16[72,1792]{1,0:T(8,128)(2,1)S(1)}, bf16[72,1792]{1,0:T(8,128)(2,1)S(1)}, bf16[72,1792]{1,0:T(8,128)(2,1)S...) custom-call(s32[1]{0:T(128)} %bitcast.me_ref, s32[16]{0:T(128)} %freq_ref.1, ...), custom_call_target="tpu_custom_call" | custom-call | flops 1792000000 | bytes 1792000000 | tf_op jit(solution)/shard_map/fourier/pallas_call | solution.py:157
  3.3 2.1 %collective-permute-start.9 = (bf16[72,1792]{1,0:T(8,128)(2,1)S(1)}, bf16[72,1792]{1,0:T(8,128)(2,1)S(1)}, u32[]{:S(2)}, u32[]{:S(2)}) collective-permute-start(bf16[72,1792]{1,0:T(8,128)(2,1)S(1)} %get-tuple-element.50), channel_id=1, source_target_pairs={{0,32},{32,64},{64,96},{96,0},{1,33},{33,65},{65,97},{97,1},{2,34}... | collective-permute-start | bytes 774152 | tf_op jit(solution)/shard_map/ppermute | solution.py:445
  5.4 2.4 %collective-permute-start.10 = (bf16[72,1792]{1,0:T(8,128)(2,1)S(1)}, bf16[72,1792]{1,0:T(8,128)(2,1)S(1)}, u32[]{:S(2)}, u32[]{:S(2)}) collective-permute-start(bf16[72,1792]{1,0:T(8,128)(2,1)S(1)} %get-tuple-element.51), channel_id=1, source_target_pairs={{0,64},{32,96},{64,0},{96,32},{1,65},{33,97},{65,1},{97,33},{2,66}... | collective-permute-start | bytes 774152 | tf_op jit(solution)/shard_map/ppermute | solution.py:445
  7.9 1.2 %collective-permute-start.11 = (bf16[72,1792]{1,0:T(8,128)(2,1)S(1)}, bf16[72,1792]{1,0:T(8,128)(2,1)S(1)}, u32[]{:S(2)}, u32[]{:S(2)}) collective-permute-start(bf16[72,1792]{1,0:T(8,128)(2,1)S(1)} %get-tuple-element.52), channel_id=1, source_target_pairs={{0,96},{32,0},{64,32},{96,64},{1,97},{33,1},{65,33},{97,65},{2,98}... | collective-permute-start | bytes 774152 | tf_op jit(solution)/shard_map/ppermute | solution.py:445
  9.0 3.8 %fourier.5 = (bf16[72,1792]{1,0:T(8,128)(2,1)S(1)}, bf16[72,1792]{1,0:T(8,128)(2,1)S(1)}, bf16[72,1792]{1,0:T(8,128)(2,1)S(1)}, bf16[72,1792]{1,0:T(8,128)(2,1)S(1)}, s32[1]{0:T(128)}) custom-call(s32[1]{0:T(128)} %bitcast.me_ref, bf16[256,1024]{1,0:T(8,128)(2,1)S(1)} %get-tuple-element.33.band_ref, bf16[32,128]{1,0:T(8,128)(2,1)S(1)} %get-tuple-element.34.edge_ref, ...), custom_call_target="tpu_custom_call" | custom-call | flops 1792000000 | bytes 1792000000 | tf_op jit(solution)/shard_map/fourier/pallas_call | solution.py:157
  12.9 0.4 collective-permute-start.6
  13.2 0.9 %collective-permute-start.7 = (bf16[72,1792]{1,0:T(8,128)(2,1)S(1)}, bf16[72,1792]{1,0:T(8,128)(2,1)S(1)}, u32[]{:S(2)}, u32[]{:S(2)}) collective-permute-start(bf16[72,1792]{1,0:T(8,128)(2,1)S(1)} %get-tuple-element.47), channel_id=1, source_target_pairs={{0,64},{32,96},{64,0},{96,32},{1,65},{33,97},{65,1},{97,33},{2,66}... | collective-permute-start | bytes 774152 | tf_op jit(solution)/shard_map/ppermute | solution.py:445
  14.1 0.0 collective-permute-done.9.refs_1_
  14.1 1.6 %collective-permute-start.8 = (bf16[72,1792]{1,0:T(8,128)(2,1)S(1)}, bf16[72,1792]{1,0:T(8,128)(2,1)S(1)}, u32[]{:S(2)}, u32[]{:S(2)}) collective-permute-start(bf16[72,1792]{1,0:T(8,128)(2,1)S(1)} %get-tuple-element.48), channel_id=1, source_target_pairs={{0,96},{32,0},{64,32},{96,64},{1,97},{33,1},{65,33},{97,65},{2,98}... | collective-permute-start | bytes 774152 | tf_op jit(solution)/shard_map/ppermute | solution.py:445
  15.7 4.6 %fourier.6 = (bf16[72,1792]{1,0:T(8,128)(2,1)S(1)}, bf16[72,1792]{1,0:T(8,128)(2,1)S(1)}, bf16[72,1792]{1,0:T(8,128)(2,1)S(1)}, bf16[72,1792]{1,0:T(8,128)(2,1)S(1)}, s32[1]{0:T(128)}) custom-call(s32[1]{0:T(128)} %get-tuple-element.35.me_ref, bf16[256,1024]{1,0:T(8,128)(2,1)S(1)} %get-tuple-element.33.band_ref, ...), custom_call_target="tpu_custom_call" | custom-call | flops 1792000000 | bytes 1792000000 | tf_op jit(solution)/shard_map/fourier/pallas_call | solution.py:157
  20.3 0.0 copy-start
  20.3 3.5 %fourier.7 = (bf16[72,768]{1,0:T(8,128)(2,1)S(1)}, bf16[72,768]{1,0:T(8,128)(2,1)S(1)}, bf16[72,768]{1,0:T(8,128)(2,1)S(1)}, bf16[72,768]{1,0:T(8,128)(2,1)S(1)}, s32[1]{0:T(128)}) custom-call(s32[1]{0:T(128)} %get-tuple-element.36.me_ref, bf16[256,1024]{1,0:T(8,128)(2,1)S(1)} %get-tuple-element.33.band_ref, bf16[32,128]{1,0:T(8,128)(2,1)S(1)} %get-tuple-element.34.edge_ref, ...), custom_call_target="tpu_custom_call" | custom-call | flops 768000000 | bytes 768000000 | tf_op jit(solution)/shard_map/fourier/pallas_call | solution.py:157
  23.8 0.0 collective-permute-done.10.refs_2_
  23.8 0.5 collective-permute-start.3
  24.3 0.0 collective-permute-done.11.refs_3_
  24.3 1.9 %collective-permute-start.4 = (bf16[72,1792]{1,0:T(8,128)(2,1)S(1)}, bf16[72,1792]{1,0:T(8,128)(2,1)S(1)}, u32[]{:S(2)}, u32[]{:S(2)}) collective-permute-start(bf16[72,1792]{1,0:T(8,128)(2,1)S(1)} %get-tuple-element.43), channel_id=1, source_target_pairs={{0,64},{32,96},{64,0},{96,32},{1,65},{33,97},{65,1},{97,33},{2,66}... | collective-permute-start | bytes 774152 | tf_op jit(solution)/shard_map/ppermute | solution.py:445
  26.2 0.4 collective-permute-done.6.refs_1_
  26.6 1.6 %collective-permute-start.5 = (bf16[72,1792]{1,0:T(8,128)(2,1)S(1)}, bf16[72,1792]{1,0:T(8,128)(2,1)S(1)}, u32[]{:S(2)}, u32[]{:S(2)}) collective-permute-start(bf16[72,1792]{1,0:T(8,128)(2,1)S(1)} %get-tuple-element.44), channel_id=1, source_target_pairs={{0,96},{32,0},{64,32},{96,64},{1,97},{33,1},{65,33},{97,65},{2,98}... | collective-permute-start | bytes 774152 | tf_op jit(solution)/shard_map/ppermute | solution.py:445
  28.2 0.0 copy-done
  28.2 1.1 %gram.4 = (f32[64,128]{1,0:T(8,128)S(1)}, bf16[256,1792]{1,0:T(8,128)(2,1)S(1)}) custom-call(s32[1]{0:T(128)} %bitcast.me_ref, f32[3,2048]{1,0:T(4,128)S(1)} %copy-done, bf16[72,1792]{1,0:T(8,128)(2,1)S(1)} %get-tuple-element.49.refs_0_, bf16[72,1792]{1,0:T(8,128)(2,1)S(1)} %collective-permute-done.9.refs_1_, ...), custom_call_target="tpu_custom_call" | custom-call | flops 1792000000 | bytes 1792000000 | tf_op jit(solution)/shard_map/gram/pallas_call | solution.py:220
  29.3 0.9 %collective-permute-done.7.refs_2_ = bf16[72,1792]{1,0:T(8,128)(2,1)S(1)} collective-permute-done((bf16[72,1792]{1,0:T(8,128)(2,1)S(1)}, bf16[72,1792]{1,0:T(8,128)(2,1)S(1)}, u32[]{:S(2)}, u32[]{:S(2)}) %collective-permute-start.7) | collective-permute-done | bytes 258080 | tf_op jit(solution)/shard_map/ppermute | solution.py:445
  30.2 0.0 collective-permute-start
  30.2 0.3 collective-permute-done.8.refs_3_
  30.4 1.8 %collective-permute-start.1 = (bf16[72,768]{1,0:T(8,128)(2,1)S(1)}, bf16[72,768]{1,0:T(8,128)(2,1)S(1)}, u32[]{:S(2)}, u32[]{:S(2)}) collective-permute-start(bf16[72,768]{1,0:T(8,128)(2,1)S(1)} %get-tuple-element.39), channel_id=1, source_target_pairs={{0,64},{32,96},{64,0},{96,32},{1,65},{33,97},{65,1},{97,33},{2,66}... | collective-permute-start | bytes 331784 | tf_op jit(solution)/shard_map/ppermute | solution.py:445
  32.2 1.1 %gram.5 = (f32[64,128]{1,0:T(8,128)S(1)}, bf16[256,1792]{1,0:T(8,128)(2,1)S(1)}) custom-call(s32[1]{0:T(128)} %bitcast.me_ref, f32[3,2048]{1,0:T(4,128)S(1)} %copy-done, bf16[72,1792]{1,0:T(8,128)(2,1)S(1)} %get-tuple-element.45.refs_0_, bf16[72,1792]{1,0:T(8,128)(2,1)S(1)} %collective-permute-done.6.refs_1_, ...), custom_call_target="tpu_custom_call" | custom-call | flops 1792000000 | bytes 1792000000 | tf_op jit(solution)/shard_map/gram/pallas_call | solution.py:220
  33.3 4.3 %collective-permute-done.3.refs_1_ = bf16[72,1792]{1,0:T(8,128)(2,1)S(1)} collective-permute-done((bf16[72,1792]{1,0:T(8,128)(2,1)S(1)}, bf16[72,1792]{1,0:T(8,128)(2,1)S(1)}, u32[]{:S(2)}, u32[]{:S(2)}) %collective-permute-start.3) | collective-permute-done | bytes 258080 | tf_op jit(solution)/shard_map/ppermute | solution.py:445
  37.7 0.0 collective-permute-start.2
  37.7 3.6 %collective-permute-done.4.refs_2_ = bf16[72,1792]{1,0:T(8,128)(2,1)S(1)} collective-permute-done((bf16[72,1792]{1,0:T(8,128)(2,1)S(1)}, bf16[72,1792]{1,0:T(8,128)(2,1)S(1)}, u32[]{:S(2)}, u32[]{:S(2)}) %collective-permute-start.4) | collective-permute-done | bytes 258080 | tf_op jit(solution)/shard_map/ppermute | solution.py:445
  41.3 0.0 collective-permute-done.5.refs_3_
  41.3 1.1 %gram.6 = (f32[64,128]{1,0:T(8,128)S(1)}, bf16[256,1792]{1,0:T(8,128)(2,1)S(1)}) custom-call(s32[1]{0:T(128)} %bitcast.me_ref, f32[3,2048]{1,0:T(4,128)S(1)} %copy-done, bf16[72,1792]{1,0:T(8,128)(2,1)S(1)} %get-tuple-element.41.refs_0_, bf16[72,1792]{1,0:T(8,128)(2,1)S(1)} %collective-permute-done.3.refs_1_, ...), custom_call_target="tpu_custom_call" | custom-call | flops 1792000000 | bytes 1792000000 | tf_op jit(solution)/shard_map/gram/pallas_call | solution.py:220
  42.4 3.2 %collective-permute-done.refs_1_ = bf16[72,768]{1,0:T(8,128)(2,1)S(1)} collective-permute-done((bf16[72,768]{1,0:T(8,128)(2,1)S(1)}, bf16[72,768]{1,0:T(8,128)(2,1)S(1)}, u32[]{:S(2)}, u32[]{:S(2)}) %collective-permute-start) | collective-permute-done | bytes 110624 | tf_op jit(solution)/shard_map/ppermute | solution.py:445
  45.5 0.5 collective-permute-done.1.refs_2_
  46.0 0.0 collective-permute-done.2.refs_3_
  46.0 0.6 gram.7
  46.6 1.6 %collective-permute-start.12 = (f32[64,128]{1,0:T(8,128)S(1)}, f32[64,128]{1,0:T(8,128)S(1)}, u32[]{:S(2)}, u32[]{:S(2)}) collective-permute-start(f32[64,128]{1,0:T(8,128)S(1)} %get-tuple-element.56), channel_id=1, source_target_pairs={{0,1},{1,0},{2,3},{3,2},{4,5},{5,4},{6,7},{7,6},{8,9},{9,8},{10,11... | collective-permute-start | bytes 98312 | tf_op jit(solution)/shard_map/ppermute | solution.py:418
  48.2 0.9 %collective-permute-done.12 = f32[64,128]{1,0:T(8,128)S(1)} collective-permute-done((f32[64,128]{1,0:T(8,128)S(1)}, f32[64,128]{1,0:T(8,128)S(1)}, u32[]{:S(2)}, u32[]{:S(2)}) %collective-permute-start.12) | collective-permute-done | bytes 32800 | tf_op jit(solution)/shard_map/ppermute | solution.py:418
  49.1 1.9 %collective-permute-start.13 = (f32[64,128]{1,0:T(8,128)S(1)}, f32[64,128]{1,0:T(8,128)S(1)}, u32[]{:S(2)}, u32[]{:S(2)}) collective-permute-start(f32[64,128]{1,0:T(8,128)S(1)} %add.15), channel_id=1, source_target_pairs={{0,3},{1,2},{2,1},{3,0},{4,7},{5,6},{6,5},{7,4},{8,11},{9,10},{10,... | collective-permute-start | bytes 98312 | tf_op jit(solution)/shard_map/ppermute | solution.py:418
  51.0 1.6 %collective-permute-done.13 = f32[64,128]{1,0:T(8,128)S(1)} collective-permute-done((f32[64,128]{1,0:T(8,128)S(1)}, f32[64,128]{1,0:T(8,128)S(1)}, u32[]{:S(2)}, u32[]{:S(2)}) %collective-permute-start.13) | collective-permute-done | bytes 32800 | tf_op jit(solution)/shard_map/ppermute | solution.py:418
  52.6 3.9 %collective-permute-start.14 = (f32[64,128]{1,0:T(8,128)S(1)}, f32[64,128]{1,0:T(8,128)S(1)}, u32[]{:S(2)}, u32[]{:S(2)}) collective-permute-start(f32[64,128]{1,0:T(8,128)S(1)} %add.16), channel_id=1, source_target_pairs={{0,7},{1,6},{2,5},{3,4},{4,3},{5,2},{6,1},{7,0},{8,15},{9,14},{10,... | collective-permute-start | bytes 98312 | tf_op jit(solution)/shard_map/ppermute | solution.py:418
  56.5 1.6 %collective-permute-done.14 = f32[64,128]{1,0:T(8,128)S(1)} collective-permute-done((f32[64,128]{1,0:T(8,128)S(1)}, f32[64,128]{1,0:T(8,128)S(1)}, u32[]{:S(2)}, u32[]{:S(2)}) %collective-permute-start.14) | collective-permute-done | bytes 32800 | tf_op jit(solution)/shard_map/ppermute | solution.py:418
  58.1 1.4 %collective-permute-start.15 = (f32[64,128]{1,0:T(8,128)S(1)}, f32[64,128]{1,0:T(8,128)S(1)}, u32[]{:S(2)}, u32[]{:S(2)}) collective-permute-start(f32[64,128]{1,0:T(8,128)S(1)} %add.17), channel_id=1, source_target_pairs={{0,9},{1,8},{2,11},{3,10},{4,13},{5,12},{6,15},{7,14},{8,1},{9,0},... | collective-permute-start | bytes 98312 | tf_op jit(solution)/shard_map/ppermute | solution.py:418
  59.4 2.0 %collective-permute-done.15 = f32[64,128]{1,0:T(8,128)S(1)} collective-permute-done((f32[64,128]{1,0:T(8,128)S(1)}, f32[64,128]{1,0:T(8,128)S(1)}, u32[]{:S(2)}, u32[]{:S(2)}) %collective-permute-start.15) | collective-permute-done | bytes 32800 | tf_op jit(solution)/shard_map/ppermute | solution.py:418
  61.4 2.8 %collective-permute-start.16 = (f32[64,128]{1,0:T(8,128)S(1)}, f32[64,128]{1,0:T(8,128)S(1)}, u32[]{:S(2)}, u32[]{:S(2)}) collective-permute-start(f32[64,128]{1,0:T(8,128)S(1)} %add.18), channel_id=1, source_target_pairs={{0,25},{1,24},{2,27},{3,26},{4,29},{5,28},{6,31},{7,30},{8,17},{9,... | collective-permute-start | bytes 98312 | tf_op jit(solution)/shard_map/ppermute | solution.py:418
  64.2 1.8 %collective-permute-done.16 = f32[64,128]{1,0:T(8,128)S(1)} collective-permute-done((f32[64,128]{1,0:T(8,128)S(1)}, f32[64,128]{1,0:T(8,128)S(1)}, u32[]{:S(2)}, u32[]{:S(2)}) %collective-permute-start.16) | collective-permute-done | bytes 32800 | tf_op jit(solution)/shard_map/ppermute | solution.py:418
  66.0 3.3 %recon.1 = bf16[4,2,3,32,2048]{4,3,2,1,0:T(8,128)(2,1)} custom-call(f32[64,128]{1,0:T(8,128)S(1)} %add.19.total_ref, bf16[256,1792]{1,0:T(8,128)(2,1)S(1)} %get-tuple-element.57.refs_0_, bf16[256,1792]{1,0:T(8,128)(2,1)S(1)} %get-tuple-element.58.refs_1_, bf16[256,1792]{1,0:T(8,128)(2,1)S(1)} %get-tuple-element.59.refs_2_, ...), custom_call_target="tpu_custom_call" | custom-call | tf_op jit(solution)/shard_map/recon/pallas_call | solution.py:385
  (5 shorter events, 0.0 us)
Async XLA Ops:
  3.3 10.8 %collective-permute-start.9 = (bf16[72,1792]{1,0:T(8,128)(2,1)S(1)}, bf16[72,1792]{1,0:T(8,128)(2,1)S(1)}, u32[]{:S(2)}, u32[]{:S(2)}) collective-permute-start(bf16[72,1792]{1,0:T(8,128)(2,1)S(1)} %get-tuple-element.50), channel_id=1, source_target_pairs={{0,32},{32,64},{64,96},{96,0},{1,33},{33,65},{65,97},{97,1},{2,34}... | collective-permute-start | bytes 774152 | tf_op jit(solution)/shard_map/ppermute | solution.py:445
  5.4 18.4 %collective-permute-start.10 = (bf16[72,1792]{1,0:T(8,128)(2,1)S(1)}, bf16[72,1792]{1,0:T(8,128)(2,1)S(1)}, u32[]{:S(2)}, u32[]{:S(2)}) collective-permute-start(bf16[72,1792]{1,0:T(8,128)(2,1)S(1)} %get-tuple-element.51), channel_id=1, source_target_pairs={{0,64},{32,96},{64,0},{96,32},{1,65},{33,97},{65,1},{97,33},{2,66}... | collective-permute-start | bytes 774152 | tf_op jit(solution)/shard_map/ppermute | solution.py:445
  7.9 16.5 %collective-permute-start.11 = (bf16[72,1792]{1,0:T(8,128)(2,1)S(1)}, bf16[72,1792]{1,0:T(8,128)(2,1)S(1)}, u32[]{:S(2)}, u32[]{:S(2)}) collective-permute-start(bf16[72,1792]{1,0:T(8,128)(2,1)S(1)} %get-tuple-element.52), channel_id=1, source_target_pairs={{0,96},{32,0},{64,32},{96,64},{1,97},{33,1},{65,33},{97,65},{2,98}... | collective-permute-start | bytes 774152 | tf_op jit(solution)/shard_map/ppermute | solution.py:445
  12.9 13.8 %collective-permute-start.6 = (bf16[72,1792]{1,0:T(8,128)(2,1)S(1)}, bf16[72,1792]{1,0:T(8,128)(2,1)S(1)}, u32[]{:S(2)}, u32[]{:S(2)}) collective-permute-start(bf16[72,1792]{1,0:T(8,128)(2,1)S(1)} %get-tuple-element.46), channel_id=1, source_target_pairs={{0,32},{32,64},{64,96},{96,0},{1,33},{33,65},{65,97},{97,1},{2,34}... | collective-permute-start | bytes 774152 | tf_op jit(solution)/shard_map/ppermute | solution.py:445
  13.2 16.9 %collective-permute-start.7 = (bf16[72,1792]{1,0:T(8,128)(2,1)S(1)}, bf16[72,1792]{1,0:T(8,128)(2,1)S(1)}, u32[]{:S(2)}, u32[]{:S(2)}) collective-permute-start(bf16[72,1792]{1,0:T(8,128)(2,1)S(1)} %get-tuple-element.47), channel_id=1, source_target_pairs={{0,64},{32,96},{64,0},{96,32},{1,65},{33,97},{65,1},{97,33},{2,66}... | collective-permute-start | bytes 774152 | tf_op jit(solution)/shard_map/ppermute | solution.py:445
  14.1 16.3 %collective-permute-start.8 = (bf16[72,1792]{1,0:T(8,128)(2,1)S(1)}, bf16[72,1792]{1,0:T(8,128)(2,1)S(1)}, u32[]{:S(2)}, u32[]{:S(2)}) collective-permute-start(bf16[72,1792]{1,0:T(8,128)(2,1)S(1)} %get-tuple-element.48), channel_id=1, source_target_pairs={{0,96},{32,0},{64,32},{96,64},{1,97},{33,1},{65,33},{97,65},{2,98}... | collective-permute-start | bytes 774152 | tf_op jit(solution)/shard_map/ppermute | solution.py:445
  20.3 7.9 %copy-start = (f32[3,2048]{1,0:T(4,128)S(1)}, f32[3,2048]{1,0:T(4,128)}, u32[]{:S(2)}) copy-start(f32[3,2048]{1,0:T(4,128)} %weight_ref.7) | copy-start | bytes 73732
  23.8 13.9 %collective-permute-start.3 = (bf16[72,1792]{1,0:T(8,128)(2,1)S(1)}, bf16[72,1792]{1,0:T(8,128)(2,1)S(1)}, u32[]{:S(2)}, u32[]{:S(2)}) collective-permute-start(bf16[72,1792]{1,0:T(8,128)(2,1)S(1)} %get-tuple-element.42), channel_id=1, source_target_pairs={{0,32},{32,64},{64,96},{96,0},{1,33},{33,65},{65,97},{97,1},{2,34}... | collective-permute-start | bytes 774152 | tf_op jit(solution)/shard_map/ppermute | solution.py:445
  24.3 16.9 %collective-permute-start.4 = (bf16[72,1792]{1,0:T(8,128)(2,1)S(1)}, bf16[72,1792]{1,0:T(8,128)(2,1)S(1)}, u32[]{:S(2)}, u32[]{:S(2)}) collective-permute-start(bf16[72,1792]{1,0:T(8,128)(2,1)S(1)} %get-tuple-element.43), channel_id=1, source_target_pairs={{0,64},{32,96},{64,0},{96,32},{1,65},{33,97},{65,1},{97,33},{2,66}... | collective-permute-start | bytes 774152 | tf_op jit(solution)/shard_map/ppermute | solution.py:445
  26.6 14.7 %collective-permute-start.5 = (bf16[72,1792]{1,0:T(8,128)(2,1)S(1)}, bf16[72,1792]{1,0:T(8,128)(2,1)S(1)}, u32[]{:S(2)}, u32[]{:S(2)}) collective-permute-start(bf16[72,1792]{1,0:T(8,128)(2,1)S(1)} %get-tuple-element.44), channel_id=1, source_target_pairs={{0,96},{32,0},{64,32},{96,64},{1,97},{33,1},{65,33},{97,65},{2,98}... | collective-permute-start | bytes 774152 | tf_op jit(solution)/shard_map/ppermute | solution.py:445
  30.2 15.4 %collective-permute-start = (bf16[72,768]{1,0:T(8,128)(2,1)S(1)}, bf16[72,768]{1,0:T(8,128)(2,1)S(1)}, u32[]{:S(2)}, u32[]{:S(2)}) collective-permute-start(bf16[72,768]{1,0:T(8,128)(2,1)S(1)} %get-tuple-element.38), channel_id=1, source_target_pairs={{0,32},{32,64},{64,96},{96,0},{1,33},{33,65},{65,97},{97,1},{2,34}... | collective-permute-start | bytes 331784 | tf_op jit(solution)/shard_map/ppermute | solution.py:445
  30.4 15.6 %collective-permute-start.1 = (bf16[72,768]{1,0:T(8,128)(2,1)S(1)}, bf16[72,768]{1,0:T(8,128)(2,1)S(1)}, u32[]{:S(2)}, u32[]{:S(2)}) collective-permute-start(bf16[72,768]{1,0:T(8,128)(2,1)S(1)} %get-tuple-element.39), channel_id=1, source_target_pairs={{0,64},{32,96},{64,0},{96,32},{1,65},{33,97},{65,1},{97,33},{2,66}... | collective-permute-start | bytes 331784 | tf_op jit(solution)/shard_map/ppermute | solution.py:445
  37.7 8.3 %collective-permute-start.2 = (bf16[72,768]{1,0:T(8,128)(2,1)S(1)}, bf16[72,768]{1,0:T(8,128)(2,1)S(1)}, u32[]{:S(2)}, u32[]{:S(2)}) collective-permute-start(bf16[72,768]{1,0:T(8,128)(2,1)S(1)} %get-tuple-element.40), channel_id=1, source_target_pairs={{0,96},{32,0},{64,32},{96,64},{1,97},{33,1},{65,33},{97,65},{2,98}... | collective-permute-start | bytes 331784 | tf_op jit(solution)/shard_map/ppermute | solution.py:445
  46.6 2.5 %collective-permute-start.12 = (f32[64,128]{1,0:T(8,128)S(1)}, f32[64,128]{1,0:T(8,128)S(1)}, u32[]{:S(2)}, u32[]{:S(2)}) collective-permute-start(f32[64,128]{1,0:T(8,128)S(1)} %get-tuple-element.56), channel_id=1, source_target_pairs={{0,1},{1,0},{2,3},{3,2},{4,5},{5,4},{6,7},{7,6},{8,9},{9,8},{10,11... | collective-permute-start | bytes 98312 | tf_op jit(solution)/shard_map/ppermute | solution.py:418
  49.1 3.5 %collective-permute-start.13 = (f32[64,128]{1,0:T(8,128)S(1)}, f32[64,128]{1,0:T(8,128)S(1)}, u32[]{:S(2)}, u32[]{:S(2)}) collective-permute-start(f32[64,128]{1,0:T(8,128)S(1)} %add.15), channel_id=1, source_target_pairs={{0,3},{1,2},{2,1},{3,0},{4,7},{5,6},{6,5},{7,4},{8,11},{9,10},{10,... | collective-permute-start | bytes 98312 | tf_op jit(solution)/shard_map/ppermute | solution.py:418
  52.6 5.5 %collective-permute-start.14 = (f32[64,128]{1,0:T(8,128)S(1)}, f32[64,128]{1,0:T(8,128)S(1)}, u32[]{:S(2)}, u32[]{:S(2)}) collective-permute-start(f32[64,128]{1,0:T(8,128)S(1)} %add.16), channel_id=1, source_target_pairs={{0,7},{1,6},{2,5},{3,4},{4,3},{5,2},{6,1},{7,0},{8,15},{9,14},{10,... | collective-permute-start | bytes 98312 | tf_op jit(solution)/shard_map/ppermute | solution.py:418
  58.1 3.3 %collective-permute-start.15 = (f32[64,128]{1,0:T(8,128)S(1)}, f32[64,128]{1,0:T(8,128)S(1)}, u32[]{:S(2)}, u32[]{:S(2)}) collective-permute-start(f32[64,128]{1,0:T(8,128)S(1)} %add.17), channel_id=1, source_target_pairs={{0,9},{1,8},{2,11},{3,10},{4,13},{5,12},{6,15},{7,14},{8,1},{9,0},... | collective-permute-start | bytes 98312 | tf_op jit(solution)/shard_map/ppermute | solution.py:418
  61.4 4.6 %collective-permute-start.16 = (f32[64,128]{1,0:T(8,128)S(1)}, f32[64,128]{1,0:T(8,128)S(1)}, u32[]{:S(2)}, u32[]{:S(2)}) collective-permute-start(f32[64,128]{1,0:T(8,128)S(1)} %add.18), channel_id=1, source_target_pairs={{0,25},{1,24},{2,27},{3,26},{4,29},{5,28},{6,31},{7,30},{8,17},{9,... | collective-permute-start | bytes 98312 | tf_op jit(solution)/shard_map/ppermute | solution.py:418
